TPU v7x, 1024 devices: a whole 8x8x8 slice. The times are simulated.
1024 devices in a mesh: dp: 16 (over x, core), node: 8 (over z), local: 8 (over y).
Axes of the slice: x: 8, y: 8, z: 8, core: 2. Of those that a mesh axis runs over, the one named last changes fastest.
Arguments:
- tokens: bfloat16 [3072, 4096], P(('node', 'local'), 'dp'), may hold values from -6 to 6
- cotangent: bfloat16 [3072, 4096], P(('node', 'local'), 'dp'), may hold values from -0.59765625 to 0.59765625
- routes: int32 [3072, 8], P(('node', 'local')), may hold values from 0 to 127, as said below
- gate_weights: float32 [3072, 8], P(('node', 'local')), may hold values from 0.1 to 0.6
- w_gate: bfloat16 [128, 4096, 1024], P(('node', 'local'), 'dp'), may hold values from -0.09375 to 0.09375
- w_up: bfloat16 [128, 4096, 1024], P(('node', 'local'), 'dp'), may hold values from -0.09375 to 0.09375
- w_down: bfloat16 [128, 1024, 4096], P(('node', 'local'), None, 'dp'), may hold values from -0.1875 to 0.1875
Outputs:
- mixed_out: bfloat16 [3072, 4096], P(('node', 'local'), 'dp')
- grad_tokens: bfloat16 [3072, 4096], P(('node', 'local'), 'dp')
- grad_gates: float32 [3072, 8], P(('node', 'local'))
Inputs may be any that keep to these rules, and one draw needn't show every extreme that they name: `routes`: each row names 8 different experts, 2 from each of 4 node groups (expert e lies in group e // 16). In each aligned block of 48 rows one node group is named by every row, and no expert is named by more than 6 rows, some exactly 6.
All inputs are finite; a program needn't handle non-finite values.
Results may differ from a plain program's by a relative error of at most 0.005.
Values may be sent and summed in bfloat16 or wider, within the bound.
A program may use at most 32 MiB of HBM per device.

v0:
```python
import jax
import jax.numpy as jnp
from jax import lax
from jax.sharding import PartitionSpec as P

BALANCE = 2.0


def route_tables(routes, experts_all, exp_dev, capacity):
    onehot = (routes[:, :, None] == lax.broadcasted_iota(jnp.int32, (1, 1, experts_all), 2)).astype(
        jnp.int32
    )
    present = jnp.sum(onehot, axis=1)
    before = jnp.cumsum(present, axis=0) - present
    slot_rank = jnp.sum(onehot * before[:, None, :], axis=2)
    target = routes // exp_dev
    local_expert = routes % exp_dev
    position = (target * capacity + slot_rank) * exp_dev + local_expert
    return (onehot, present, position)


def body(tokens, cotangent, routes, gate_weights, w_gate, w_up, w_down):
    token_count, features = tokens.shape
    fanout = routes.shape[1]
    exp_dev = w_gate.shape[0]
    node_count = lax.axis_size("node")
    local_count = lax.axis_size("local")
    peer_count = node_count * local_count
    limit_groups = node_count // 2
    capacity = token_count * (fanout // limit_groups) // (exp_dev * local_count)
    experts_all = exp_dev * peer_count
    slot_total = peer_count * capacity
    buffer_size = slot_total * exp_dev
    onehot, present, position = route_tables(routes, experts_all, exp_dev, capacity)
    flat_position = position.reshape(-1)
    hits = (flat_position[:, None] == lax.broadcasted_iota(jnp.int32, (1, buffer_size), 1)).astype(
        jnp.int32
    )
    pair_token = lax.broadcasted_iota(jnp.int32, (token_count * fanout, 1), 0) // fanout
    source = jnp.sum(hits * (pair_token + 1), axis=0) - 1
    source = jnp.where(source < 0, token_count, source)
    paired = jnp.concatenate([tokens, cotangent], axis=1)
    padded = jnp.concatenate([paired, jnp.zeros((1, 2 * features), paired.dtype)], axis=0)
    outgoing = jnp.take(padded, source, axis=0)
    outgoing = outgoing.reshape(peer_count, capacity, exp_dev, 2 * features)
    load_share = jnp.sum(present, axis=0).astype(jnp.bfloat16).reshape(peer_count, exp_dev)
    arrived, load_rows = (
        lax.all_to_all(outgoing, ("node", "local"), split_axis=0, concat_axis=0, tiled=True),
        lax.all_to_all(load_share, ("node", "local"), split_axis=0, concat_axis=0, tiled=True),
    )
    expert_load = jnp.sum(load_rows.astype(jnp.float32), axis=0)
    received = arrived.reshape(slot_total, exp_dev, 2 * features)
    gate_part = jnp.einsum(
        "sej,ejh->seh", received[:, :, :features], w_gate, preferred_element_type=jnp.float32
    )
    up_part = jnp.einsum(
        "sej,ejh->seh", received[:, :, :features], w_up, preferred_element_type=jnp.float32
    )
    back_part = jnp.einsum(
        "sej,ehj->seh", received[:, :, features:], w_down, preferred_element_type=jnp.float32
    )
    summed = lax.psum_scatter(
        jnp.stack([gate_part, up_part, back_part], axis=2), "dp", scatter_dimension=0, tiled=True
    )
    gate_sum = summed[:, :, 0]
    up_sum = summed[:, :, 1]
    back_sum = summed[:, :, 2]
    logistic = jax.nn.sigmoid(gate_sum)
    active = gate_sum * logistic
    hidden = (active * up_sum).astype(jnp.bfloat16)
    d_gate = (back_sum * up_sum * logistic * (1.0 + gate_sum * (1.0 - logistic))).astype(
        jnp.bfloat16
    )
    d_up = (back_sum * active).astype(jnp.bfloat16)
    shares = jnp.stack([hidden, d_gate, d_up], axis=2)
    piece_rows = lax.all_gather(shares, "dp", axis=0, tiled=True)
    forward_part = jnp.einsum(
        "seh,ehj->sej", piece_rows[:, :, 0], w_down, preferred_element_type=jnp.float32
    )
    input_part = jnp.einsum(
        "seh,ejh->sej", piece_rows[:, :, 1], w_gate, preferred_element_type=jnp.float32
    )
    input_part = input_part + jnp.einsum(
        "seh,ejh->sej", piece_rows[:, :, 2], w_up, preferred_element_type=jnp.float32
    )
    results = jnp.concatenate([forward_part, input_part], axis=2)
    results = results.reshape(peer_count, capacity, exp_dev, 2 * features)
    totals = jnp.broadcast_to(expert_load[None, :], (peer_count, exp_dev))
    returned, all_loads = (
        lax.all_to_all(results, ("node", "local"), split_axis=0, concat_axis=0, tiled=True),
        lax.all_to_all(totals, ("node", "local"), split_axis=0, concat_axis=0, tiled=True),
    )
    picked = jnp.take(returned.reshape(buffer_size, 2 * features), flat_position, axis=0)
    picked = picked.reshape(token_count, fanout, 2 * features)
    forward_rows = picked[:, :, :features]
    input_rows = picked[:, :, features:]
    weights = gate_weights[:, :, None]
    mixed_out = jnp.sum(weights * forward_rows, axis=1).astype(jnp.bfloat16)
    grad_tokens = jnp.sum(weights * input_rows, axis=1).astype(jnp.bfloat16)
    partial_dot = jnp.sum(cotangent.astype(jnp.float32)[:, None, :] * forward_rows, axis=2)
    inner_dot = lax.psum(partial_dot, "dp")
    frequency = all_loads.reshape(experts_all) * experts_all / (fanout * token_count * peer_count)
    named_frequency = jnp.sum(onehot.astype(jnp.float32) * frequency[None, None, :], axis=2)
    grad_gates = inner_dot + BALANCE * named_frequency
    return (mixed_out, grad_tokens, grad_gates)


def solution(mesh):
    placed = (
        P(("node", "local"), "dp"),
        P(("node", "local"), "dp"),
        P(("node", "local"), None),
        P(("node", "local"), None),
        P(("node", "local"), "dp", None),
        P(("node", "local"), "dp", None),
        P(("node", "local"), None, "dp"),
    )
    return jax.shard_map(
        body,
        mesh=mesh,
        in_specs=placed,
        out_specs=(
            P(("node", "local"), "dp"),
            P(("node", "local"), "dp"),
            P(("node", "local"), None),
        ),
        check_vma=False,
    )
```

profile of v0, /device:TPU:1, one launch (start us, length us, event | category | flops | bytes accessed | tf_op | source)
XLA Modules:
  0.0 314.7 jit_solution(18329395229386491595)
XLA Ops:
  7.2 0.0 copy-start
  7.2 0.0 reduce-scatter.2.cloned.1.call-start
  7.2 0.8 copy.49
  8.1 0.1 convert_reduce_fusion.1
  8.2 0.1 reduce_window_sum.11
  8.3 1.0 convert_reduce_fusion
  9.3 0.1 copy.50
  9.3 0.7 compare_and_fusion.1
  10.0 0.1 copy.52
  10.1 0.1 reshape.181
  10.2 0.2 select_reduce_fusion
  10.4 0.1 sub.35
  10.6 0.8 fusion.15
  11.4 2.7 gather_fusion
  14.0 0.3 gather.13
  14.3 0.1 compare_and_fusion
  14.5 1.0 broadcast_select_fusion
  15.5 45.6 %all_to_all.22 = bf16[64,6,2,512]{3,2,1,0:T(2,128)(2,1)S(1)} all-to-all(bf16[64,6,2,512]{3,2,1,0:T(2,128)(2,1)S(1)} %broadcast_select_fusion), channel_id=1, replica_groups=mesh['dp'=16,'node'=8,'local'=8] {'node','local'}, dimensions={0} | all-to-all | bytes 1572864 | tf_op jit(solution)/shard_map/all_to_all | solution.py:48
  61.1 0.0 copy-start.1
  61.1 0.5 fusion.31
  61.6 0.0 copy-done
  61.6 0.6 convolution_bitcast_fusion.1
  62.2 0.1 copy-done.1
  62.3 0.0 copy-start.2
  62.3 0.6 convolution_bitcast_fusion.2
  62.9 0.6 copy-done.2
  63.5 0.6 convolution_bitcast_fusion
  64.1 4.6 %pad_maximum_fusion = f32[384,2,3,1024]{3,0,1,2:T(8,128)} fusion(f32[384,2,1,1024]{3,0,1,2:T(8,128)S(1)} %convolution_bitcast_fusion, f32[384,2,1,1024]{3,0,1,2:T(8,128)S(1)} %convolution_bitcast_fusion.1, f32[384,2,1,1024]{3,0,1,2:T(8,128)S(1)} %convolution_bitcast_fusion.2), kind=kLoop, calls=%fused_computation.2 | loop fusion | flops 4718592 | bytes 18874368 | tf_op jit(solution)/shard_map/stack | solution.py:63
  68.7 0.0 reduce-scatter.2.cloned.1.call-update
  68.8 0.0 all-gather.2.cloned.1.call-start
  68.8 73.8 %reduce-scatter.2.cloned.1.call-done = f32[24,2,3,1024]{3,0,1,2:T(8,128)} async-done(((f32[384,2,3,1024]{3,0,1,2:T(8,128)}), f32[24,2,3,1024]{3,0,1,2:T(8,128)}) %reduce-scatter.2.cloned.1.call-update) | async-done | bytes 589840 | tf_op jit(solution)/shard_map/reduce_scatter | solution.py:62
  142.7 1.2 multiply_convert_fusion.2
  143.9 0.7 pad_maximum_fusion.2
  144.6 0.0 all-gather.2.cloned.1.call-update
  144.7 0.2 convert_element_type.57
  144.8 23.0 %all_to_all.23 = bf16[64,1,2]{2,1,0:T(2,128)(2,1)S(1)} all-to-all(bf16[64,1,2]{2,1,0:T(2,128)(2,1)S(1)} %convert_element_type.57), channel_id=1, replica_groups=mesh['dp'=16,'node'=8,'local'=8] {'node','local'}, dimensions={0} | all-to-all | bytes 512 | tf_op jit(solution)/shard_map/all_to_all | solution.py:49
  167.8 0.1 convert_reduce_fusion.2
  167.9 0.6 broadcast_in_dim.44
  168.5 4.5 %all-to-all-start.3 = ((f32[64,1,2]{2,1,0:T(1,128)}), f32[64,1,2]{2,1,0:T(1,128)S(1)}, u32[]{:S(2)}, u32[]{:S(2)}) async-start(f32[64,1,2]{2,1,0:T(1,128)} %broadcast_in_dim.44), calls=%async_computation.4 | async-start | bytes 65536 | tf_op jit(solution)/shard_map/all_to_all | solution.py:91
  173.0 21.8 %all-gather.2.cloned.1.call-done = bf16[384,2,3,1024]{3,0,1,2:T(8,128)(2,1)} async-done(((bf16[24,2,3,1024]{3,0,1,2:T(8,128)(2,1)}), bf16[384,2,3,1024]{3,0,1,2:T(8,128)(2,1)}) %all-gather.2.cloned.1.call-update) | async-done | bytes 4718608 | tf_op jit(solution)/shard_map/all_gather | solution.py:76
  194.9 2.1 fusion
  197.0 2.2 fusion.3
  199.2 2.1 fusion.5
  201.3 0.1 pad_maximum_fusion.1
  201.5 0.0 copy-start.3
  201.5 0.0 copy-start.4
  201.5 2.1 copy.56
  203.6 0.0 all-to-all-done.3
  203.6 14.3 %all-to-all-start.1 = ((f32[64,6,2,512]{3,2,1,0:T(2,128)}), f32[64,6,2,512]{3,2,1,0:T(2,128)}, u32[]{:S(2)}, u32[]{:S(2)}) async-start(f32[64,6,2,512]{3,2,1,0:T(2,128)} %bitcast.12), calls=%async_computation.2 | async-start | bytes 3145728 | tf_op jit(solution)/shard_map/all_to_all | solution.py:90
  217.9 0.1 reshape.185
  217.9 0.0 copy-done.3
  218.0 0.1 copy.51
  218.1 0.0 copy-done.4
  218.1 0.1 copy.48
  218.2 0.1 multiply_reduce_fusion.2
  218.3 0.1 div.40
  218.4 0.2 fusion.11
  218.6 38.4 %all-to-all-done.1 = f32[64,6,2,512]{3,2,1,0:T(2,128)} async-done(((f32[64,6,2,512]{3,2,1,0:T(2,128)}), f32[64,6,2,512]{3,2,1,0:T(2,128)}, u32[]{:S(2)}, u32[]{:S(2)}) %all-to-all-start.1) | async-done | bytes 1572896 | tf_op jit(solution)/shard_map/all_to_all | solution.py:90
  257.0 2.4 reshape.184
  259.4 1.6 gather_fusion.1
  261.0 0.1 bitcast_select_fusion
  261.1 0.9 fusion.6
  262.0 45.2 %psum.7 = f32[48,8]{1,0:T(8,128)S(1)} all-reduce(f32[48,8]{1,0:T(8,128)S(1)} %get-tuple-element.14), channel_id=1, replica_groups=mesh['dp'=16,'node'=8,'local'=8] {'dp'}, use_global_device_ids=true, to_apply=%region_8.9 | all-reduce | flops 384 | bytes 3072 | tf_op jit(solution)/shard_map/psum | solution.py:101
  307.2 0.7 copy.59
  (10 shorter events, 0.1 us)
Async XLA Ops:
  7.2 54.5 %copy-start = (bf16[2,256,1024]{2,1,0:T(8,128)(2,1)S(1)}, bf16[2,256,1024]{2,1,0:T(8,128)(2,1)}, u32[]{:S(2)}) copy-start(bf16[2,256,1024]{2,1,0:T(8,128)(2,1)} %param.12) | copy-start | bytes 3145732
  7.2 135.5 %reduce-scatter.2.cloned.1.call-start = ((), (), s32[]{:S(2)}) async-start(), calls=%async_computation.5 | async-start | bytes 10027008 | tf_op jit(solution)/shard_map/reduce_scatter | solution.py:62
  61.1 1.2 copy-start.1
  62.3 1.2 copy-start.2
  68.8 126.1 %all-gather.2.cloned.1.call-start = ((), (), s32[]{:S(2)}) async-start(), calls=%async_computation.6 | async-start | bytes 5013504 | tf_op jit(solution)/shard_map/all_gather | solution.py:76
  168.5 35.1 %all-to-all-start.3 = ((f32[64,1,2]{2,1,0:T(1,128)}), f32[64,1,2]{2,1,0:T(1,128)S(1)}, u32[]{:S(2)}, u32[]{:S(2)}) async-start(f32[64,1,2]{2,1,0:T(1,128)} %broadcast_in_dim.44), calls=%async_computation.4 | async-start | bytes 65536 | tf_op jit(solution)/shard_map/all_to_all | solution.py:91
  201.5 16.5 %copy-start.3 = (bf16[48,256]{1,0:T(8,128)(2,1)S(1)}, bf16[48,256]{1,0:T(8,128)(2,1)}, u32[]{:S(2)}) copy-start(bf16[48,256]{1,0:T(8,128)(2,1)} %param.8) | copy-start | bytes 73732
  201.5 16.6 %copy-start.4 = (f32[48,8]{0,1:T(8,128)S(1)}, f32[48,8]{0,1:T(8,128)}, u32[]{:S(2)}) copy-start(f32[48,8]{0,1:T(8,128)} %param.10) | copy-start | bytes 4612
  203.6 53.4 %all-to-all-start.1 = ((f32[64,6,2,512]{3,2,1,0:T(2,128)}), f32[64,6,2,512]{3,2,1,0:T(2,128)}, u32[]{:S(2)}, u32[]{:S(2)}) async-start(f32[64,6,2,512]{3,2,1,0:T(2,128)} %bitcast.12), calls=%async_computation.2 | async-start | bytes 3145728 | tf_op jit(solution)/shard_map/all_to_all | solution.py:90
Sparse Core Ops, SparseCore 0:
  68.9 73.7 reduce-scatter.1
  145.4 49.4 all-gather.1
where the time goes:
time: 317 us; the launch traced here: 315 us
  waiting for transfers between devices  134 us (42%)
  blocking collectives  114 us (36%)
  starting transfers between devices  18.9 us (6%)
  between operations  14.3 us (5%)
  local copies, waits for them, and re-layouts  13.4 us (4%)
  other arithmetic  12.1 us (4%)
  matrix products  8.21 us (3%)
    reduce_scatter x1, waiting for transfers between devices, body(): lax.psum_scatter(jnp.stack([gate_part, up_part, back_part], axis=2), 'dp'...  73.8 us
    all_to_all x1, blocking collectives, body(): lax.all_to_all(outgoing, ('node', 'local'), split_axis=0, concat_axis=0,...  45.6 us
    psum x1, blocking collectives, body(): inner_dot = lax.psum(partial_dot, 'dp')  45.2 us
    all_to_all x1, waiting for transfers between devices, body(): lax.all_to_all(results, ('node', 'local'), split_axis=0, concat_axis=0, t...  38.4 us
    all_to_all x1, blocking collectives, body(): lax.all_to_all(load_share, ('node', 'local'), split_axis=0, concat_axis=0...  23 us
    all_gather x1, waiting for transfers between devices, body(): piece_rows = lax.all_gather(shares, 'dp', axis=0, tiled=True)  21.8 us
    all_to_all x1, starting transfers between devices, body(): lax.all_to_all(results, ('node', 'local'), split_axis=0, concat_axis=0, t...  14.3 us
  transfers between devices with their start and end apart: 4, of which 3 were waited for; matrix products, arithmetic and copies ran while one was open for 3% of the time, Pallas kernels for 0%

commit v1 on v0

v1 whole, which is shorter than its diff:
```python
import functools

import jax
import jax.numpy as jnp
from jax import lax
from jax.experimental import pallas as pl
from jax.experimental.pallas import tpu as pltpu
from jax.sharding import PartitionSpec as P

BALANCE = 2.0
CAP = 6
SUBS = 4
STEPS = 32766.0
MESH = pl.DeviceIdType.MESH
F32, BF16 = jnp.float32, jnp.bfloat16
VMEM = pl.BlockSpec(memory_space=pltpu.VMEM)
ANY = pl.BlockSpec(memory_space=pl.ANY)
LIMIT = 56 * 1024 * 1024


def greet(peers):
    barrier = pltpu.get_barrier_semaphore()
    for peer in peers:
        pl.semaphore_signal(barrier, inc=1, device_id=peer, device_id_type=MESH)
    pl.semaphore_wait(barrier, len(peers))


def push(src, dst, send, recv, peer):
    copy = pltpu.make_async_remote_copy(
        src_ref=src, dst_ref=dst, send_sem=send, recv_sem=recv, device_id=peer, device_id_type=MESH
    )
    copy.start()
    return copy


def other_core():
    core = lax.rem(lax.axis_index("dp"), 2)
    return core, lax.axis_index("dp") + 1 - 2 * core


def spread_kernel(nodes, tok, cot, meta, wg, wu, wd, tokz, cotz, metaz, wg2, wu2, wd2, send, recv, wsend, wrecv):
    me = lax.axis_index("node")
    core, twin = other_core()
    peers = [{"node": lax.rem(me + step, nodes)} for step in range(1, nodes)]
    greet(peers + [{"dp": twin}])
    copies = []
    for step in range(1, nodes):
        for index, (src, dst) in enumerate(((meta, metaz), (tok, tokz), (cot, cotz))):
            copies.append(push(src, dst.at[me], send.at[step - 1, index], recv.at[step - 1, index], peers[step - 1]))
    for index, (src, dst) in enumerate(((wg, wg2), (wu, wu2), (wd, wd2))):
        copies.append(push(src.at[1 - core], dst, wsend.at[index], wrecv.at[index], {"dp": twin}))
    tokz[me] = tok[...]
    cotz[me] = cot[...]
    metaz[me] = meta[...]
    for copy in copies:
        copy.wait()


def spread(nodes, tok, cot, meta, wg, wu, wd):
    arrays = (tok, cot, meta)
    weights = (wg, wu, wd)
    return pl.pallas_call(
        functools.partial(spread_kernel, nodes),
        out_shape=[jax.ShapeDtypeStruct((nodes,) + a.shape, a.dtype) for a in arrays]
        + [jax.ShapeDtypeStruct(a.shape[1:], a.dtype) for a in weights],
        in_specs=[VMEM] * 3 + [ANY] * 3,
        out_specs=[VMEM] * 3 + [ANY] * 3,
        scratch_shapes=[pltpu.SemaphoreType.DMA((nodes - 1, 3))] * 2 + [pltpu.SemaphoreType.DMA((3,))] * 2,
        compiler_params=pltpu.CompilerParams(collective_id=0, has_side_effects=True, vmem_limit_bytes=LIMIT),
    )(tok, cot, meta, wg, wu, wd)


def slot_codes(rows, experts, top, routes):
    columns = routes.shape[1]
    base = (lax.axis_index("node") * experts).astype(F32)
    name = lax.broadcasted_iota(jnp.int32, (experts, columns), 0).astype(F32) + base
    chosen = jnp.zeros((experts, columns), F32)
    for k in range(top):
        chosen = chosen + jnp.where(routes[k : k + 1, :] == name, 1.0, 0.0)
    scale = -(-32768 // rows)
    earlier = lax.broadcasted_iota(jnp.int32, (columns, columns), 0)
    later = lax.broadcasted_iota(jnp.int32, (columns, columns), 1)
    block_row = (earlier * scale) >> 15
    block_col = (later * scale) >> 15
    before = jnp.where((block_row == block_col) & (earlier < later), 1.0, 0.0).astype(BF16)
    rank = jnp.dot(chosen.astype(BF16), before, preferred_element_type=F32)
    block = (lax.broadcasted_iota(jnp.int32, (experts, columns), 1) * scale >> 15).astype(F32)
    code = jnp.where(chosen > 0.0, block * CAP + rank, -1.0)
    return name, chosen, code


def lay_out(metaz, top, rows):
    nodes = metaz.shape[0]
    weights = jnp.concatenate([metaz[i, :top, :rows] for i in range(nodes)], axis=1)
    routes = jnp.concatenate([metaz[i, top : 2 * top, :rows] for i in range(nodes)], axis=1)
    return weights, routes


def select_kernel(top, tokz, cotz, metaz, tok_out, cot_out, count_out):
    nodes, rows, features = tokz.shape
    experts, slots, _ = tok_out.shape
    _, routes = lay_out(metaz, top, rows)
    _, chosen, code = slot_codes(rows, experts, top, routes)
    columns = routes.shape[1]
    place = lax.broadcasted_iota(jnp.int32, (1, slots, 1), 1).astype(F32)
    pick = jnp.where(code[:, None, :] == place, 1.0, 0.0).astype(BF16).reshape(experts * slots, columns)
    for src, dst in ((tokz, tok_out), (cotz, cot_out)):
        got = jnp.dot(pick, src[...].reshape(columns, features), preferred_element_type=F32)
        dst[...] = got.astype(BF16).reshape(experts, slots, features)
    count_out[...] = jnp.broadcast_to(jnp.sum(chosen, axis=1, keepdims=True), count_out.shape)


def select(experts, top, tokz, cotz, metaz):
    nodes, rows, features = tokz.shape
    slots = nodes * CAP
    shape = jax.ShapeDtypeStruct((experts, slots, features), BF16)
    return pl.pallas_call(
        functools.partial(select_kernel, top),
        out_shape=[shape, shape, jax.ShapeDtypeStruct((experts, 128), F32)],
        in_specs=[VMEM] * 3,
        out_specs=[VMEM] * 3,
        compiler_params=pltpu.CompilerParams(vmem_limit_bytes=LIMIT),
    )(tokz, cotz, metaz)


def slots_kernel(locals_, tok, cot, count, tok_in, cot_in, count_sum, counts, send, recv, csend, crecv, near):
    me = lax.axis_index("local")
    core, twin = other_core()
    where = [lax.rem(me + step, locals_) for step in range(locals_)]
    same = [{"local": place} for place in where]
    cross = [{"local": place, "dp": twin} for place in where]
    greet(same[1:] + cross)
    copies = []
    for step in range(locals_):
        for far, peer in ((0, same[step]), (1, cross[step])):
            if step == 0 and far == 0:
                continue
            expert = 2 * where[step] + (core if far == 0 else 1 - core)
            for index, (src, dst) in enumerate(((tok, tok_in), (cot, cot_in))):
                at = (step, far, index)
                copies.append(push(src.at[expert], dst.at[far, me], send.at[at], recv.at[at], peer))
        if step > 0:
            copies.append(push(count, counts.at[me], csend.at[step - 1], crecv.at[step - 1], same[step]))
    mine = 2 * me + core
    own = []
    for index, (src, dst) in enumerate(((tok, tok_in), (cot, cot_in))):
        own.append(pltpu.make_async_copy(src.at[mine], dst.at[0, me], near.at[index]))
        own[-1].start()
    counts[me] = count[...]
    for copy in own + copies:
        copy.wait()
    count_sum[...] = jnp.sum(counts[...], axis=0)


def slots_exchange(locals_, tok, cot, count):
    experts, slots, features = tok.shape
    shape = jax.ShapeDtypeStruct((2, locals_, slots, features), BF16)
    return pl.pallas_call(
        functools.partial(slots_kernel, locals_),
        out_shape=[shape, shape, jax.ShapeDtypeStruct(count.shape, F32)],
        in_specs=[VMEM] * 3,
        out_specs=[VMEM] * 3,
        scratch_shapes=[pltpu.VMEM((locals_,) + count.shape, F32)]
        + [pltpu.SemaphoreType.DMA((locals_, 2, 2))] * 2
        + [pltpu.SemaphoreType.DMA((max(locals_ - 1, 1),))] * 2
        + [pltpu.SemaphoreType.DMA((2,))],
        compiler_params=pltpu.CompilerParams(collective_id=1, has_side_effects=True, vmem_limit_bytes=LIMIT),
    )(tok, cot, count)


NT = (((1,), (1,)), ((), ()))


def first_kernel(chips, core, tok, cot, wg, wu, wd, wg2, wu2, wd2, out, table):
    width = wg.shape[2]

    @pl.when(pl.program_id(0) == 0)
    def _():
        table[...] = jnp.zeros_like(table)

    gate = jnp.dot(tok[0], wg[0], preferred_element_type=F32) + jnp.dot(tok[1], wg2[...], preferred_element_type=F32)
    up = jnp.dot(tok[0], wu[0], preferred_element_type=F32) + jnp.dot(tok[1], wu2[...], preferred_element_type=F32)
    back = lax.dot_general(cot[0], wd[0], NT, preferred_element_type=F32)
    back = back + lax.dot_general(cot[1], wd2[...], NT, preferred_element_type=F32)
    for index, value in enumerate((gate, up, back)):
        out[0, :, index * width : (index + 1) * width] = value
        top = jnp.max(jnp.abs(value).reshape(chips, -1, width), axis=1)
        table[index] = jnp.maximum(table[index], jnp.max(top, axis=1, keepdims=True))


def first(chips, core, tok, cot, wg, wu, wd, wg2, wu2, wd2):
    _, rows, features = tok.shape
    hidden = wg.shape[2]
    width = hidden // SUBS
    whole = pl.BlockSpec((2, rows, features), lambda s, core: (0, 0, 0))
    return pl.pallas_call(
        functools.partial(first_kernel, chips),
        out_shape=[
            jax.ShapeDtypeStruct((SUBS, rows, 3 * width), F32),
            jax.ShapeDtypeStruct((3, chips, 128), F32),
        ],
        grid_spec=pltpu.PrefetchScalarGridSpec(
            num_scalar_prefetch=1,
            grid=(SUBS,),
            in_specs=[
                whole,
                whole,
                pl.BlockSpec((1, features, width), lambda s, core: (core[0], 0, s)),
                pl.BlockSpec((1, features, width), lambda s, core: (core[0], 0, s)),
                pl.BlockSpec((1, width, features), lambda s, core: (core[0], s, 0)),
                pl.BlockSpec((features, width), lambda s, core: (0, s)),
                pl.BlockSpec((features, width), lambda s, core: (0, s)),
                pl.BlockSpec((width, features), lambda s, core: (s, 0)),
            ],
            out_specs=[
                pl.BlockSpec((1, rows, 3 * width), lambda s, core: (s, 0, 0)),
                pl.BlockSpec((3, chips, 128), lambda s, core: (0, 0, 0)),
            ],
        ),
        compiler_params=pltpu.CompilerParams(vmem_limit_bytes=LIMIT),
    )(core, tok, cot, wg, wu, wd, wg2, wu2, wd2)


def ring_kernel(
    chips, part, table, shares, values, got, stage, bounds, bounds_in, rsend, rrecv, gsend, grecv, vsend, vrecv, tsend, trecv
):
    dp = lax.axis_index("dp")
    core = lax.rem(dp, 2)
    me = (dp - core) // 2
    depth = chips // 2
    half = SUBS // 2
    width = part.shape[3] // 3
    rows = part.shape[2]

    def chip(offset):
        return lax.rem(me + offset + 2 * chips, chips)

    way = [{"dp": 2 * chip(1) + core}, {"dp": 2 * chip(-1) + core}]
    sign = (1, -1)
    greet(way)

    def halves(direction):
        return range(half) if direction == 0 else range(half, SUBS)

    copies = []

    def bound(ref, chunk):
        lines = [jnp.broadcast_to(ref[index, pl.ds(chunk, 1), :], (1, 128)) for index in range(3)]
        return jnp.concatenate([line for line in lines for _ in range(width // 128)], axis=1)

    def reduce_send(direction, step, sub, total, chunk):
        at = (direction, step, sub)
        limit = bound(bounds.at[direction, step], chunk)
        inverse = jnp.where(limit > 1e-30, STEPS / jnp.maximum(limit, 1e-30), 0.0)
        stage[at] = jnp.round(total * inverse).astype(jnp.int32).astype(jnp.int16)
        copies.append(push(stage.at[at], got.at[at], rsend.at[at], rrecv.at[at], way[direction]))

    def reduce_wait(direction, step, sub, chunk):
        at = (direction, step, sub)
        pltpu.make_async_copy(got.at[at], got.at[at], rrecv.at[at]).wait()
        limit = bound(bounds_in.at[direction, step], chunk)
        return got[at].astype(jnp.int32).astype(F32) * (limit * (1.0 / STEPS))

    def bound_send(direction, step):
        at = (direction, step)
        copies.append(push(bounds.at[at], bounds_in.at[at], tsend.at[at], trecv.at[at], way[direction]))

    def bound_wait(direction, step):
        at = (direction, step)
        pltpu.make_async_copy(bounds_in.at[at], bounds_in.at[at], trecv.at[at]).wait()

    for direction in range(2):
        bounds[direction, 0] = table[...]
        bound_send(direction, 0)
    for index in range(half):
        for direction in range(2):
            sub = halves(direction)[index]
            chunk = chip(sign[direction] * depth)
            reduce_send(direction, 0, sub, part[sub, chunk], chunk)
    for step in range(1, depth):
        for direction in range(2):
            bound_wait(direction, step - 1)
            bounds[direction, step] = table[...] + bounds_in[direction, step - 1]
            bound_send(direction, step)
        for index in range(half):
            for direction in range(2):
                if step == 1:
                    sub = halves(1 - direction)[index]
                    chunk = chip(sign[direction] * (depth - 1))
                    reduce_send(direction, 1, sub, part[sub, chunk], chunk)
        for sub in range(SUBS):
            for direction in range(2):
                if step == 1 and sub not in halves(direction):
                    continue
                chunk = chip(sign[direction] * (depth - step))
                total = part[sub, chunk] + reduce_wait(direction, step - 1, sub, chunk)
                reduce_send(direction, step, sub, total, chunk)
    for direction in range(2):
        bound_wait(direction, depth - 1)

    def gather_send(direction, step, sub):
        chunk = shares.at[sub, chip(-sign[direction] * step)]
        at = (direction, step, sub)
        copies.append(push(chunk, chunk, gsend.at[at], grecv.at[at], way[direction]))

    def gather_wait(direction, step, sub):
        chunk = shares.at[sub, chip(-sign[direction] * (step + 1))]
        pltpu.make_async_copy(chunk, chunk, grecv.at[direction, step, sub]).wait()

    def value_send(direction, step):
        chunk = values.at[chip(-sign[direction] * step)]
        at = (direction, step)
        copies.append(push(chunk, chunk, vsend.at[at], vrecv.at[at], way[direction]))

    def value_wait(direction, step):
        chunk = values.at[chip(-sign[direction] * (step + 1))]
        pltpu.make_async_copy(chunk, chunk, vrecv.at[direction, step]).wait()

    inner = jnp.zeros((rows, 1), F32)
    for index in range(half):
        for sub in (halves(0)[index], halves(1)[index]):
            total = part[sub, me]
            for direction in range(2):
                if depth > 1 or sub in halves(direction):
                    total = total + reduce_wait(direction, depth - 1, sub, me)
            gate, up, back = total[:, :width], total[:, width : 2 * width], total[:, 2 * width :]
            logistic = 1.0 / (1.0 + jnp.exp(-gate))
            active = gate * logistic
            hidden = (active * up).astype(BF16)
            shares[sub, me, :, :width] = hidden
            d_gate = back * up * logistic * (1.0 + gate * (1.0 - logistic))
            shares[sub, me, :, width : 2 * width] = d_gate.astype(BF16)
            shares[sub, me, :, 2 * width :] = (back * active).astype(BF16)
            for direction in range(2):
                if depth > 1 or sub in halves(direction):
                    gather_send(direction, 0, sub)
            inner = inner + jnp.sum(hidden.astype(F32) * back, axis=1, keepdims=True)
    lanes = lax.broadcasted_iota(jnp.int32, (rows, 128), 1)
    diagonal = lax.broadcasted_iota(jnp.int32, (rows, 128), 0) == lanes
    line = jnp.sum(jnp.where(diagonal, inner, 0.0), axis=0, keepdims=True)
    values[me] = jnp.broadcast_to(line, (8, 128))
    for direction in range(2):
        if depth > 1 or direction == 0:
            value_send(direction, 0)
    for step in range(1, depth + 1):
        last = step == depth
        for index in range(half):
            for sub in (halves(0)[index], halves(1)[index]):
                for direction in range(2):
                    if last and sub not in halves(direction):
                        continue
                    gather_wait(direction, step - 1, sub)
                    if not last and (step < depth - 1 or sub in halves(direction)):
                        gather_send(direction, step, sub)
        for direction in range(2):
            if last and direction == 1:
                continue
            value_wait(direction, step - 1)
            if not last and (step < depth - 1 or direction == 0):
                value_send(direction, step)
    for copy in copies:
        copy.wait_send()


def ring(chips, part, table):
    _, _, rows, wide = part.shape
    depth = chips // 2
    return pl.pallas_call(
        functools.partial(ring_kernel, chips),
        out_shape=[jax.ShapeDtypeStruct(part.shape, BF16), jax.ShapeDtypeStruct((chips, 8, 128), F32)],
        in_specs=[VMEM] * 2,
        out_specs=[VMEM] * 2,
        scratch_shapes=[pltpu.VMEM((2, depth, SUBS, rows, wide), jnp.int16)] * 2
        + [pltpu.VMEM((2, depth) + table.shape, F32)] * 2
        + [pltpu.SemaphoreType.DMA((2, depth, SUBS))] * 4
        + [pltpu.SemaphoreType.DMA((2, depth))] * 4,
        compiler_params=pltpu.CompilerParams(collective_id=2, has_side_effects=True, vmem_limit_bytes=LIMIT),
    )(part, table)


def second_kernel(core, shares, wg, wu, wd, wg2, wu2, wd2, out):
    features = wg2.shape[0]
    width = wg2.shape[1] // SUBS
    for side, (gate, up, down) in enumerate(((wg.at[0], wu.at[0], wd.at[0]), (wg2, wu2, wd2))):
        forward = jnp.zeros(out.shape[1:2] + (features,), F32)
        back = forward
        for sub in range(SUBS):
            units = slice(sub * width, (sub + 1) * width)
            forward = forward + jnp.dot(shares[sub, :, :width], down[units, :], preferred_element_type=F32)
            back = back + lax.dot_general(
                shares[sub, :, width : 2 * width], gate[:, units], NT, preferred_element_type=F32
            )
            back = back + lax.dot_general(shares[sub, :, 2 * width :], up[:, units], NT, preferred_element_type=F32)
        out[side, :, :features] = forward.astype(BF16)
        out[side, :, features:] = back.astype(BF16)


def second(core, shares, wg, wu, wd, wg2, wu2, wd2):
    _, rows, wide = shares.shape
    features, hidden = wg2.shape
    side = pl.BlockSpec((features, hidden), lambda i, core: (0, 0))
    return pl.pallas_call(
        second_kernel,
        out_shape=jax.ShapeDtypeStruct((2, rows, 2 * features), BF16),
        grid_spec=pltpu.PrefetchScalarGridSpec(
            num_scalar_prefetch=1,
            grid=(1,),
            in_specs=[
                pl.BlockSpec((SUBS, rows, wide), lambda i, core: (0, 0, 0)),
                pl.BlockSpec((1, features, hidden), lambda i, core: (core[0], 0, 0)),
                pl.BlockSpec((1, features, hidden), lambda i, core: (core[0], 0, 0)),
                pl.BlockSpec((1, hidden, features), lambda i, core: (core[0], 0, 0)),
                side,
                side,
                pl.BlockSpec((hidden, features), lambda i, core: (0, 0)),
            ],
            out_specs=pl.BlockSpec((2, rows, 2 * features), lambda i, core: (0, 0, 0)),
        ),
        compiler_params=pltpu.CompilerParams(vmem_limit_bytes=LIMIT),
    )(core, shares, wg, wu, wd, wg2, wu2, wd2)


def return_kernel(locals_, rows, values, back, vback, send, recv, near):
    me = lax.axis_index("local")
    core, twin = other_core()
    where = [lax.rem(me + step, locals_) for step in range(locals_)]
    same = [{"local": place} for place in where]
    cross = [{"local": place, "dp": twin} for place in where]
    greet(same[1:] + cross)
    mine = 2 * me + core
    copies = []
    for step in range(locals_):
        for far, peer in ((0, same[step]), (1, cross[step])):
            if step == 0 and far == 0:
                continue
            at = (step, far)
            copies.append(push(rows.at[far, where[step]], back.at[mine], send.at[at + (0,)], recv.at[at + (0,)], peer))
            copies.append(push(values.at[where[step]], vback.at[mine], send.at[at + (1,)], recv.at[at + (1,)], peer))
    own = pltpu.make_async_copy(rows.at[0, me], back.at[mine], near)
    own.start()
    vback[mine] = values[me]
    own.wait()
    for copy in copies:
        copy.wait()


def give_back(locals_, rows, values):
    _, _, slots, wide = rows.shape
    return pl.pallas_call(
        functools.partial(return_kernel, locals_),
        out_shape=[
            jax.ShapeDtypeStruct((2 * locals_, slots, wide), BF16),
            jax.ShapeDtypeStruct((2 * locals_, 8, 128), F32),
        ],
        in_specs=[VMEM] * 2,
        out_specs=[VMEM] * 2,
        scratch_shapes=[pltpu.SemaphoreType.DMA((locals_, 2, 2))] * 2 + [pltpu.SemaphoreType.DMA],
        compiler_params=pltpu.CompilerParams(collective_id=3, has_side_effects=True, vmem_limit_bytes=LIMIT),
    )(rows, values)


def combine_kernel(top, scale, metaz, back, vback, count, out, gates_out):
    nodes = metaz.shape[0]
    experts, slots, wide = back.shape
    rows = out.shape[1]
    columns = nodes * rows
    weights, routes = lay_out(metaz, top, rows)
    name, _, code = slot_codes(rows, experts, top, routes)
    weight = jnp.zeros((experts, columns), F32)
    for k in range(top):
        weight = weight + jnp.where(routes[k : k + 1, :] == name, weights[k : k + 1, :], 0.0)
    place = lax.broadcasted_iota(jnp.int32, (1, slots, 1), 1).astype(F32)
    hit = code[:, None, :] == place
    rows_back = back[...].reshape(experts * slots, wide)
    high = weight.astype(BF16).astype(F32)
    total = jnp.zeros((columns, wide), F32)
    for share in (high, weight - high):
        spread_ = jnp.where(hit, share[:, None, :], 0.0).astype(BF16).reshape(experts * slots, columns)
        total = total + lax.dot_general(spread_, rows_back, (((0,), (0,)), ((), ())), preferred_element_type=F32)
    out[...] = total.astype(BF16).reshape(nodes, rows, wide)
    lanes = lax.broadcasted_iota(jnp.int32, (experts, slots, 128), 2)
    diagonal = lax.broadcasted_iota(jnp.int32, (experts, slots, 128), 1) == lanes
    value = jnp.sum(jnp.where(diagonal, vback[:, 0:1, :], 0.0), axis=2, keepdims=True)
    inner = jnp.sum(jnp.where(hit, value, 0.0), axis=1)
    inner = inner + BALANCE * scale * count[:, 0:1]
    gates = [
        jnp.sum(jnp.where(routes[k : k + 1, :] == name, inner, 0.0), axis=0, keepdims=True) for k in range(top)
    ]
    gates = jnp.concatenate(gates, axis=0)
    gates_out[...] = jnp.zeros_like(gates_out)
    for i in range(nodes):
        gates_out[i, :, :rows] = gates[:, i * rows : (i + 1) * rows]


def combine(top, scale, rows, metaz, back, vback, count):
    nodes = metaz.shape[0]
    return pl.pallas_call(
        functools.partial(combine_kernel, top, scale),
        out_shape=[
            jax.ShapeDtypeStruct((nodes, rows, back.shape[2]), BF16),
            jax.ShapeDtypeStruct((nodes, top, 128), F32),
        ],
        in_specs=[VMEM] * 4,
        out_specs=[VMEM] * 2,
        compiler_params=pltpu.CompilerParams(vmem_limit_bytes=LIMIT),
    )(metaz, back, vback, count)


def finish_kernel(nodes, rows, gates, mixed, grads, gates_out, got, got_gates, send, recv):
    me = lax.axis_index("node")
    where = [lax.rem(me + step, nodes) for step in range(nodes)]
    peers = [{"node": place} for place in where]
    greet(peers[1:])
    copies = []
    for step in range(1, nodes):
        for index, (src, dst) in enumerate(((rows, got), (gates, got_gates))):
            at = (step - 1, index)
            copies.append(push(src.at[where[step]], dst.at[step - 1], send.at[at], recv.at[at], peers[step]))
    for copy in copies:
        copy.wait()
    total = rows[me].astype(F32)
    gate = gates[me]
    for step in range(nodes - 1):
        total = total + got[step].astype(F32)
        gate = gate + got_gates[step]
    features = mixed.shape[1]
    mixed[...] = total[:, :features].astype(BF16)
    grads[...] = total[:, features:].astype(BF16)
    gates_out[...] = gate


def finish(rows, gates):
    nodes, count, wide = rows.shape
    half = jax.ShapeDtypeStruct((count, wide // 2), BF16)
    return pl.pallas_call(
        functools.partial(finish_kernel, nodes),
        out_shape=[half, half, jax.ShapeDtypeStruct(gates.shape[1:], F32)],
        in_specs=[VMEM] * 2,
        out_specs=[VMEM] * 3,
        scratch_shapes=[pltpu.VMEM((nodes - 1,) + rows.shape[1:], BF16), pltpu.VMEM((nodes - 1,) + gates.shape[1:], F32)]
        + [pltpu.SemaphoreType.DMA((nodes - 1, 2))] * 2,
        compiler_params=pltpu.CompilerParams(collective_id=4, has_side_effects=True, vmem_limit_bytes=LIMIT),
    )(rows, gates)


def body(chips, nodes, locals_, tokens, cotangent, routes, gate_weights, w_gate, w_up, w_down):
    rows, features = tokens.shape
    top = routes.shape[1]
    experts = 2 * locals_
    slots = nodes * CAP
    meta = jnp.concatenate([gate_weights.T, routes.T.astype(F32)], axis=0)
    meta = jnp.pad(meta, ((0, 0), (0, 128 - rows)))
    core = lax.rem(lax.axis_index("dp"), 2).astype(jnp.int32).reshape(1)
    tokz, cotz, metaz, *swapped = spread(nodes, tokens, cotangent, meta, w_gate, w_up, w_down)
    weights = (w_gate, w_up, w_down, *swapped)
    tok, cot, count = select(experts, top, tokz, cotz, metaz)
    tok, cot, count = slots_exchange(locals_, tok, cot, count)
    tok = tok.reshape(2, locals_ * slots, features)
    cot = cot.reshape(2, locals_ * slots, features)
    part, table = first(chips, core, tok, cot, *weights)
    shares, values = ring(chips, part.reshape(SUBS, chips, locals_ * slots // chips, part.shape[2]), table)
    out = second(core, shares.reshape(part.shape), *weights)
    back, vback = give_back(locals_, out.reshape(2, locals_, slots, 2 * features), values)
    scale = experts * nodes / (top * rows * nodes * locals_)
    summed, gates = combine(top, scale, rows, metaz, back, vback, count)
    mixed, grads, gates = finish(summed, gates)
    return mixed, grads, gates[:, :rows].T


def solution(mesh):
    chips, nodes, locals_ = mesh.shape["dp"] // 2, mesh.shape["node"], mesh.shape["local"]
    placed = (
        P(("node", "local"), "dp"),
        P(("node", "local"), "dp"),
        P(("node", "local"), None),
        P(("node", "local"), None),
        P(("node", "local"), "dp", None),
        P(("node", "local"), "dp", None),
        P(("node", "local"), None, "dp"),
    )
    return jax.shard_map(
        functools.partial(body, chips, nodes, locals_),
        mesh=mesh,
        in_specs=placed,
        out_specs=(
            P(("node", "local"), "dp"),
            P(("node", "local"), "dp"),
            P(("node", "local"), None),
        ),
        check_vma=False,
    )
```

time: 317 us -> 189 us (0.60)
  Pallas kernels: 0 us -> 181 us
  waiting for transfers between devices: 134 us -> 0 us
  blocking collectives: 114 us -> 0 us
  starting transfers between devices: 18.9 us -> 0 us
  between operations: 14.3 us -> 0.68 us
  other arithmetic: 12.1 us -> 1.98 us
  local copies, waits for them, and re-layouts: 13.4 us -> 3.95 us
  matrix products: 8.21 us -> 0 us
    pallas_call x0 -> x9, Pallas kernels: none -> 181 us  [the longest x1 54.6 us: ring(): pl.pallas_call(functools.partial(ring_kernel, chips), out_shape=[jax.Shap...]
    reduce_scatter x1 -> x0, waiting for transfers between devices: 73.8 us -> none  [body(): lax.psum_scatter(jnp.stack([gate_part, up_part, back_part], axis=2), 'dp'...]
    all_to_all x2 -> x0, blocking collectives: 68.6 us -> none  [the longest x1 45.6 us: body(): lax.all_to_all(outgoing, ('node', 'local'), split_axis=0, concat_axis=0,...]
    psum x1 -> x0, blocking collectives: 45.2 us -> none  [body(): inner_dot = lax.psum(partial_dot, 'dp')]
    all_to_all x2 -> x0, waiting for transfers between devices: 38.4 us -> none  [the longest x1 38.4 us: body(): lax.all_to_all(results, ('node', 'local'), split_axis=0, concat_axis=0, t...]
    all_gather x1 -> x0, waiting for transfers between devices: 21.8 us -> none  [body(): piece_rows = lax.all_gather(shares, 'dp', axis=0, tiled=True)]
    all_to_all x2 -> x0, starting transfers between devices: 18.8 us -> none  [the longest x1 14.3 us: body(): lax.all_to_all(results, ('node', 'local'), split_axis=0, concat_axis=0, t...]
    dot_general x6 -> x0, matrix products: 8.21 us -> none  [the longest x1 2.18 us: body(): jnp.einsum('seh,ehj->sej', piece_rows[:, :, 0], w_down, preferred_element...]
  transfers between devices with their start and end apart: 4 -> 0, of which waited for: 3 -> 0; matrix products, arithmetic and copies ran while one was open for 3% -> 0% of each run, Pallas kernels for 0% -> 0%
where the time goes in v1:
time: 189 us; the launch traced here: 188 us
  Pallas kernels  181 us (96%)
  local copies, waits for them, and re-layouts  3.95 us (2%)
  other arithmetic  1.98 us (1%)
    pallas_call x1, Pallas kernels, ring(): pl.pallas_call(functools.partial(ring_kernel, chips), out_shape=[jax.Shap...  54.6 us
    pallas_call x1, Pallas kernels, slots_exchange(): pl.pallas_call(functools.partial(slots_kernel, locals_), out_shape=[shape...  31.9 us
    pallas_call x1, Pallas kernels, give_back(): pl.pallas_call(functools.partial(return_kernel, locals_), out_shape=[jax....  31.2 us
    pallas_call x1, Pallas kernels, spread(): pl.pallas_call(functools.partial(spread_kernel, nodes), out_shape=[jax.Sh...  28.5 us
    pallas_call x1, Pallas kernels, finish(): pl.pallas_call(functools.partial(finish_kernel, nodes), out_shape=[half,...  17.9 us
    pallas_call x1, Pallas kernels, first(): pl.pallas_call(functools.partial(first_kernel, chips), out_shape=[jax.Sha...  6.24 us
    pallas_call x1, Pallas kernels, second(): pl.pallas_call(second_kernel, out_shape=jax.ShapeDtypeStruct((2, rows, 2...  4.82 us

profile of v1, /device:TPU:1, one launch (start us, length us, event | category | flops | bytes accessed | tf_op | source)
XLA Modules:
  0.0 187.5 jit_solution(11333359508387236369)
XLA Ops:
  0.6 0.7 convert_bitcast_fusion
  1.3 1.3 select_maximum_fusion.meta
  2.6 28.5 %shard_map.94 = (bf16[8,48,256]{2,1,0:T(8,128)(2,1)}, bf16[8,48,256]{2,1,0:T(8,128)(2,1)}, f32[8,16,128]{2,1,0:T(8,128)}, bf16[256,1024]{1,0:T(8,128)(2,1)}, bf1...) custom-call(bf16[48,256]{1,0:T(8,128)(2,1)} %tok.1, bf16[48,256]{1,0:T(8,128)(2,1)} %cot.1, ...), custom_call_target="tpu_custom_call" | custom-call | tf_op jit(solution)/shard_map/pallas_call | solution.py:62
  31.2 2.7 %shard_map.95 = (bf16[16,48,256]{2,1,0:T(8,128)(2,1)}, bf16[16,48,256]{2,1,0:T(8,128)(2,1)}, f32[16,128]{1,0:T(8,128)}) custom-call(bf16[8,48,256]{2,1,0:T(8,128)(2,1)} %get-tuple-element.27.tokz, bf16[8,48,256]{2,1,0:T(8,128)(2,1)} %get-tuple-element.28.cotz, f32[8,16,128]{2,1,0:T(8,128)} %get-tuple-element.26.metaz), custom_call_target="tpu_custom_call" | custom-call | tf_op jit(solution)/shard_map/pallas_call | solution.py:117
  33.9 31.9 %shard_map.96 = (bf16[2,8,48,256]{3,2,1,0:T(8,128)(2,1)}, bf16[2,8,48,256]{3,2,1,0:T(8,128)(2,1)}, f32[16,128]{1,0:T(8,128)}) custom-call(bf16[16,48,256]{2,1,0:T(8,128)(2,1)} %get-tuple-element.29.tok, bf16[16,48,256]{2,1,0:T(8,128)(2,1)} %get-tuple-element.30.cot, f32[16,128]{1,0:T(8,128)} %get-tuple-element.31.count), custom_call_target="tpu_custom_call" | custom-call | tf_op jit(solution)/shard_map/pallas_call | solution.py:158
  65.8 6.2 %shard_map.97 = (f32[4,384,768]{2,1,0:T(8,128)}, f32[3,8,128]{2,1,0:T(8,128)}) custom-call(s32[1]{0:T(128)} %bitcast.2.core, bf16[2,384,256]{2,1,0:T(8,128)(2,1)} %bitcast.14, bf16[2,384,256]{2,1,0:T(8,128)(2,1)} %bitcast.15, bf16[2,256,1024]{2,1,0:T(8,128)(2,1)} %wg.5, bf16[2,256,1024]{2,1,0:T(8,128)(2,1)} %wu.5, bf16[2,1024,256]{2,1,0:T(8,128)(2,1)} %wd.5, ...), custom_call_target="tpu_custom_call" | custom-call | tf_op jit(solution)/shard_map/pallas_call | solution.py:196
  72.0 54.6 %shard_map.98 = (bf16[4,8,48,768]{3,2,1,0:T(8,128)(2,1)}, f32[8,8,128]{2,1,0:T(8,128)}) custom-call(f32[4,8,48,768]{3,2,1,0:T(8,128)} %bitcast.11, f32[3,8,128]{2,1,0:T(8,128)} %get-tuple-element.38.table), custom_call_target="tpu_custom_call" | custom-call | tf_op jit(solution)/shard_map/pallas_call | solution.py:368
  126.6 4.8 %shard_map.99 = bf16[2,384,512]{2,1,0:T(8,128)(2,1)} custom-call(s32[1]{0:T(128)} %bitcast.2.core, bf16[4,384,768]{2,1,0:T(8,128)(2,1)} %bitcast.13, bf16[2,256,1024]{2,1,0:T(8,128)(2,1)} %wg.5, bf16[2,256,1024]{2,1,0:T(8,128)(2,1)} %wu.5, bf16[2,1024,256]{2,1,0:T(8,128)(2,1)} %wd.5, bf16[256,1024]{1,0:T(8,128)(2,1)} %get-tuple-element.34.wg2, ...), custom_call_target="tpu_custom_call" | custom-call | tf_op jit(solution)/shard_map/pallas_call | solution.py:402
  131.4 31.2 %shard_map.100 = (bf16[16,48,512]{2,1,0:T(8,128)(2,1)}, f32[16,8,128]{2,1,0:T(8,128)}) custom-call(bf16[2,8,48,512]{3,2,1,0:T(8,128)(2,1)} %bitcast.12, f32[8,8,128]{2,1,0:T(8,128)} %get-tuple-element.40.values), custom_call_target="tpu_custom_call" | custom-call | tf_op jit(solution)/shard_map/pallas_call | solution.py:449
  162.6 3.0 %shard_map.101 = (bf16[8,48,512]{2,1,0:T(8,128)(2,1)}, f32[8,8,128]{2,1,0:T(8,128)}) custom-call(f32[8,16,128]{2,1,0:T(8,128)} %get-tuple-element.26.metaz, bf16[16,48,512]{2,1,0:T(8,128)(2,1)} %get-tuple-element.41.back, f32[16,8,128]{2,1,0:T(8,128)} %get-tuple-element.42.vback, f32[16,128]{1,0:T(8,128)} %get-tuple-element.43.count), custom_call_target="tpu_custom_call" | custom-call | tf_op jit(solution)/shard_map/pallas_call | solution.py:497
  165.6 17.9 %shard_map.102 = (bf16[48,256]{1,0:T(8,128)(2,1)}, bf16[48,256]{1,0:T(8,128)(2,1)}, f32[8,128]{1,0:T(8,128)}) custom-call(bf16[8,48,512]{2,1,0:T(8,128)(2,1)} %get-tuple-element.44.rows, f32[8,8,128]{2,1,0:T(8,128)} %get-tuple-element.45.gates), custom_call_target="tpu_custom_call" | custom-call | tf_op jit(solution)/shard_map/pallas_call | solution.py:535
  183.6 1.3 slice_bitcast_fusion
  184.9 1.3 copy.12
  186.2 1.3 copy.13

commit v2 on v1

v2 whole, which is shorter than its diff:
```python
import functools

import jax
import jax.numpy as jnp
from jax import lax
from jax.experimental import pallas as pl
from jax.experimental.pallas import tpu as pltpu
from jax.sharding import PartitionSpec as P

BALANCE = 2.0
CAP = 6
USUAL = 32
SUBS = 4
STEPS = 32766.0
MESH = pl.DeviceIdType.MESH
F32, BF16 = jnp.float32, jnp.bfloat16
VMEM = pl.BlockSpec(memory_space=pltpu.VMEM)
ANY = pl.BlockSpec(memory_space=pl.ANY)
LIMIT = 56 * 1024 * 1024


def greet(peers):
    barrier = pltpu.get_barrier_semaphore()
    for peer in peers:
        pl.semaphore_signal(barrier, inc=1, device_id=peer, device_id_type=MESH)
    pl.semaphore_wait(barrier, len(peers))


def push(src, dst, send, recv, peer):
    copy = pltpu.make_async_remote_copy(
        src_ref=src, dst_ref=dst, send_sem=send, recv_sem=recv, device_id=peer, device_id_type=MESH
    )
    copy.start()
    return copy


def other_core():
    core = lax.rem(lax.axis_index("dp"), 2)
    return core, lax.axis_index("dp") + 1 - 2 * core


def upright(line, rows):
    lanes = lax.broadcasted_iota(jnp.int32, (rows, line.shape[-1]), 1)
    diagonal = lax.broadcasted_iota(jnp.int32, (rows, line.shape[-1]), 0) == lanes
    return jnp.sum(jnp.where(diagonal, line, 0.0), axis=1, keepdims=True)


def lying(column, lanes):
    rows = column.shape[0]
    lane = lax.broadcasted_iota(jnp.int32, (rows, lanes), 1)
    diagonal = lax.broadcasted_iota(jnp.int32, (rows, lanes), 0) == lane
    return jnp.sum(jnp.where(diagonal, column, 0.0), axis=0, keepdims=True)


def ring_of(axis, size):
    me = lax.axis_index(axis)
    return me, [lax.rem(me + step, size) for step in range(size)]


def spread_kernel(
    nodes, locals_, tok, cot, gates, routes, wg, wu, wd, tokz, cotl, metaz, metal, wg2, wu2, wd2,
    meta, send, recv, wsend, wrecv,
):
    node, nodes_at = ring_of("node", nodes)
    place, locals_at = ring_of("local", locals_)
    core, twin = other_core()
    top = gates.shape[1]
    for k in range(top):
        meta[k : k + 1, :] = lying(gates[:, k : k + 1], 128)
        meta[top + k : top + k + 1, :] = lying(routes[:, k : k + 1].astype(F32), 128)
    far = [{"node": at} for at in nodes_at]
    side = [{"local": at} for at in locals_at]
    greet(far[1:] + side[1:] + [{"dp": twin}])
    copies = []
    for step in range(1, max(nodes, locals_)):
        for path, (peers, me, arrays) in enumerate(
            ((far, node, ((meta, metaz), (tok, tokz))), (side, place, ((meta, metal), (cot, cotl))))
        ):
            if step < len(peers):
                for index, (src, dst) in enumerate(arrays):
                    at = (path, step - 1, index)
                    copies.append(push(src, dst.at[me], send.at[at], recv.at[at], peers[step]))
    for index, (src, dst) in enumerate(((wg, wg2), (wu, wu2), (wd, wd2))):
        copies.append(push(src.at[1 - core], dst, wsend.at[index], wrecv.at[index], {"dp": twin}))
    tokz[node] = tok[...]
    cotl[place] = cot[...]
    metaz[node] = meta[...]
    metal[place] = meta[...]
    for copy in copies:
        copy.wait()


def spread(nodes, locals_, tok, cot, gates, routes, wg, wu, wd):
    most = max(nodes, locals_) - 1
    meta = (2 * gates.shape[1], 128)
    return pl.pallas_call(
        functools.partial(spread_kernel, nodes, locals_),
        out_shape=[
            jax.ShapeDtypeStruct((nodes,) + tok.shape, BF16),
            jax.ShapeDtypeStruct((locals_,) + cot.shape, BF16),
            jax.ShapeDtypeStruct((nodes,) + meta, F32),
            jax.ShapeDtypeStruct((locals_,) + meta, F32),
        ]
        + [jax.ShapeDtypeStruct(a.shape[1:], a.dtype) for a in (wg, wu, wd)],
        in_specs=[VMEM] * 4 + [ANY] * 3,
        out_specs=[VMEM] * 4 + [ANY] * 3,
        scratch_shapes=[pltpu.VMEM(meta, F32)]
        + [pltpu.SemaphoreType.DMA((2, most, 2))] * 2
        + [pltpu.SemaphoreType.DMA((3,))] * 2,
        compiler_params=pltpu.CompilerParams(collective_id=0, has_side_effects=True, vmem_limit_bytes=LIMIT),
    )(tok, cot, gates, routes, wg, wu, wd)


def names_of(path, nodes, locals_):
    if path == 0:
        return lax.broadcasted_iota(jnp.int32, (2 * locals_, 1), 0) + 2 * locals_ * lax.axis_index("node")
    order = lax.broadcasted_iota(jnp.int32, (2 * nodes, 1), 0)
    return (order >> 1) * (2 * locals_) + (order & 1) + 2 * lax.axis_index("local")


def slot_codes(rows, top, routes, names):
    columns = routes.shape[1]
    experts = names.shape[0]
    name = jnp.broadcast_to(names.astype(F32), (experts, columns))
    chosen = jnp.zeros((experts, columns), F32)
    for k in range(top):
        chosen = chosen + jnp.where(routes[k : k + 1, :] == name, 1.0, 0.0)
    scale = -(-32768 // rows)
    earlier = lax.broadcasted_iota(jnp.int32, (columns, columns), 0)
    later = lax.broadcasted_iota(jnp.int32, (columns, columns), 1)
    block_row = (earlier * scale) >> 15
    block_col = (later * scale) >> 15
    before = jnp.where((block_row == block_col) & (earlier < later), 1.0, 0.0).astype(BF16)
    rank = jnp.dot(chosen.astype(BF16), before, preferred_element_type=F32)
    block = (lax.broadcasted_iota(jnp.int32, (experts, columns), 1) * scale >> 15).astype(F32)
    code = jnp.where(chosen > 0.0, block * CAP + rank, -1.0)
    return name, chosen, code


def lay_out(meta, top, rows):
    blocks = meta.shape[0]
    weights = jnp.concatenate([meta[i, :top, :rows] for i in range(blocks)], axis=1)
    routes = jnp.concatenate([meta[i, top : 2 * top, :rows] for i in range(blocks)], axis=1)
    return weights, routes


def select_kernel(top, nodes, locals_, tokz, cotl, metaz, metal, tok_out, cot_out, count_out):
    rows, features = tokz.shape[1:]
    for path, (src, meta, dst) in enumerate(((tokz, metaz, tok_out), (cotl, metal, cot_out))):
        experts, slots, _ = dst.shape
        _, routes = lay_out(meta, top, rows)
        columns = routes.shape[1]
        _, chosen, code = slot_codes(rows, top, routes, names_of(path, nodes, locals_))
        place = lax.broadcasted_iota(jnp.int32, (1, slots, 1), 1).astype(F32)
        pick = jnp.where(code[:, None, :] == place, 1.0, 0.0).astype(BF16).reshape(experts * slots, columns)
        got = jnp.dot(pick, src[...].reshape(columns, features), preferred_element_type=F32)
        dst[...] = got.astype(BF16).reshape(experts, slots, features)
        if path == 0:
            block = (lax.broadcasted_iota(jnp.int32, (columns, 128), 0) * -(-32768 // rows)) >> 15
            by_block = jnp.where(block == lax.broadcasted_iota(jnp.int32, (columns, 128), 1), 1.0, 0.0).astype(BF16)
            count_out[:experts, :] = jnp.dot(chosen.astype(BF16), by_block, preferred_element_type=F32)
            total = 2 * nodes * locals_
            name = lax.broadcasted_iota(jnp.int32, (total, columns), 0).astype(F32)
            hits = jnp.zeros((total, columns), F32)
            for k in range(top):
                hits = hits + jnp.where(routes[k : k + 1, :] == name, 1.0, 0.0)
            count_out[experts:, :] = jnp.broadcast_to(lying(jnp.sum(hits, axis=1, keepdims=True), 128), (8, 128))


def select(top, nodes, locals_, tokz, cotl, metaz, metal):
    features = tokz.shape[2]
    return pl.pallas_call(
        functools.partial(select_kernel, top, nodes, locals_),
        out_shape=[
            jax.ShapeDtypeStruct((2 * locals_, nodes * CAP, features), BF16),
            jax.ShapeDtypeStruct((2 * nodes, locals_ * CAP, features), BF16),
            jax.ShapeDtypeStruct((2 * locals_ + 8, 128), F32),
        ],
        in_specs=[VMEM] * 4,
        out_specs=[VMEM] * 3,
        compiler_params=pltpu.CompilerParams(vmem_limit_bytes=LIMIT),
    )(tokz, cotl, metaz, metal)


def paths_of(nodes, locals_):
    core, twin = other_core()
    ways = []
    for axis, size in (("local", locals_), ("node", nodes)):
        me, at = ring_of(axis, size)
        ways.append((me, at, [{axis: one} for one in at], [{axis: one, "dp": twin} for one in at]))
    peers = ways[0][2][1:] + ways[1][2][1:] + ways[0][3] + ways[1][3][1:]
    return core, ways, peers


def slots_kernel(nodes, locals_, tok, cot, count, tok_in, cot_in, counts, count_sum, send, recv, csend, crecv):
    core, ways, everyone = paths_of(nodes, locals_)
    greet(everyone)
    copies = []
    for step in range(1, locals_):
        copies.append(
            push(count, counts.at[ways[0][0]], csend.at[step - 1], crecv.at[step - 1], ways[0][2][step])
        )
    for step in list(range(1, max(nodes, locals_))) + [0]:
        for path, ((me, at, same, cross), src, dst) in enumerate(zip(ways, (tok, cot), (tok_in, cot_in))):
            for far, peers in enumerate((same, cross)):
                if step >= len(at) or (step == 0 and far == 0):
                    continue
                expert = 2 * at[step] + (core if far == 0 else 1 - core)
                sem = (path, step, far)
                copies.append(push(src.at[expert], dst.at[far, me], send.at[sem], recv.at[sem], peers[step]))
    for (me, _, _, _), src, dst in zip(ways, (tok, cot), (tok_in, cot_in)):
        dst[0, me] = src[2 * me + core]
    counts[ways[0][0]] = count[...]
    for copy in copies:
        copy.wait()
    count_sum[...] = jnp.sum(counts[...], axis=0)


def slots_exchange(nodes, locals_, tok, cot, count):
    most = max(nodes, locals_)
    return pl.pallas_call(
        functools.partial(slots_kernel, nodes, locals_),
        out_shape=[
            jax.ShapeDtypeStruct((2, locals_) + tok.shape[1:], BF16),
            jax.ShapeDtypeStruct((2, nodes) + cot.shape[1:], BF16),
            jax.ShapeDtypeStruct((locals_,) + count.shape, F32),
            jax.ShapeDtypeStruct(count.shape, F32),
        ],
        in_specs=[VMEM] * 3,
        out_specs=[VMEM] * 4,
        scratch_shapes=[pltpu.SemaphoreType.DMA((2, most, 2))] * 2 + [pltpu.SemaphoreType.DMA((locals_,))] * 2,
        compiler_params=pltpu.CompilerParams(collective_id=1, has_side_effects=True, vmem_limit_bytes=LIMIT),
    )(tok, cot, count)


NT = (((1,), (1,)), ((), ()))


def places(nodes, locals_, counts):
    slots = nodes * locals_ * CAP
    index = lax.broadcasted_iota(jnp.int32, (locals_, slots), 1).astype(F32)
    axis = lax.broadcasted_iota(jnp.int32, (locals_, slots), 0).astype(F32)
    lane = lax.broadcasted_iota(jnp.int32, (128, slots), 0).astype(F32)
    earlier = lax.broadcasted_iota(jnp.int32, (slots, slots), 0).astype(F32)
    rows, valid = [], None
    for path, inner in enumerate((nodes, locals_)):
        major = jnp.floor((index + 0.5) * (1.0 / (CAP * inner)))
        within = index - major * (CAP * inner)
        minor = jnp.floor((within + 0.5) * (1.0 / CAP))
        rank = within - minor * CAP
        of_node, of_local = (minor, major) if path == 0 else (major, minor)
        by_node = jnp.where(lane == of_node[:1, :], 1.0, 0.0).astype(BF16)
        count = jnp.dot(counts.astype(BF16), by_node, preferred_element_type=F32)
        count = jnp.sum(jnp.where(axis == of_local, count, 0.0), axis=0, keepdims=True)
        filled = rank[:1, :] < count
        if path == 0:
            valid = jnp.broadcast_to(jnp.where(filled, 1.0, 0.0), (8, slots)).astype(BF16)
        first_path = of_local[:1, :] * (CAP * nodes) + of_node[:1, :] * CAP + rank[:1, :]
        before = jnp.where(earlier < first_path, 1.0, 0.0).astype(BF16)
        row = jnp.dot(valid, before, preferred_element_type=F32)[:1, :]
        rows.append(jnp.where(filled, row, -1.0))
    return rows


def first_kernel(chips, nodes, locals_, at, counts, tok, cot, wg, wu, wd, wg2, wu2, wd2, out, table, rows_of):
    width = wg.shape[2]
    rows = out.shape[1]
    slots = tok.shape[1]

    @pl.when(pl.program_id(0) == 0)
    def _():
        table[...] = jnp.zeros_like(table)
        own = counts[:, pl.ds(at[1], 1), :].reshape(locals_, 128)
        row = lax.broadcasted_iota(jnp.int32, (rows, slots), 0).astype(F32)
        for path, (place, src) in enumerate(zip(places(nodes, locals_, own), (tok, cot))):
            pack = jnp.where(row == place, 1.0, 0.0).astype(BF16)
            for side in range(2):
                rows_of[path, side] = jnp.dot(pack, src[side], preferred_element_type=F32).astype(BF16)

    gate = jnp.dot(rows_of[0, 0], wg[0], preferred_element_type=F32)
    gate = gate + jnp.dot(rows_of[0, 1], wg2[...], preferred_element_type=F32)
    up = jnp.dot(rows_of[0, 0], wu[0], preferred_element_type=F32)
    up = up + jnp.dot(rows_of[0, 1], wu2[...], preferred_element_type=F32)
    back = lax.dot_general(rows_of[1, 0], wd[0], NT, preferred_element_type=F32)
    back = back + lax.dot_general(rows_of[1, 1], wd2[...], NT, preferred_element_type=F32)
    for index, value in enumerate((gate, up, back)):
        out[0, :, index * width : (index + 1) * width] = value
        top = jnp.max(jnp.abs(value).reshape(chips, -1, width), axis=1)
        table[index] = jnp.maximum(table[index], jnp.max(top, axis=1, keepdims=True))


def first(chips, nodes, locals_, rows, at, counts, tok, cot, wg, wu, wd, wg2, wu2, wd2):
    _, slots, features = tok.shape
    hidden = wg.shape[2]
    width = hidden // SUBS
    whole = pl.BlockSpec((2, slots, features), lambda s, at: (0, 0, 0))
    return pl.pallas_call(
        functools.partial(first_kernel, chips, nodes, locals_),
        out_shape=[
            jax.ShapeDtypeStruct((SUBS, rows, 3 * width), F32),
            jax.ShapeDtypeStruct((3, chips, 128), F32),
        ],
        grid_spec=pltpu.PrefetchScalarGridSpec(
            num_scalar_prefetch=1,
            grid=(SUBS,),
            in_specs=[
                pl.BlockSpec(counts.shape, lambda s, at: (0, 0, 0)),
                whole,
                whole,
                pl.BlockSpec((1, features, width), lambda s, at: (at[0], 0, s)),
                pl.BlockSpec((1, features, width), lambda s, at: (at[0], 0, s)),
                pl.BlockSpec((1, width, features), lambda s, at: (at[0], s, 0)),
                pl.BlockSpec((features, width), lambda s, at: (0, s)),
                pl.BlockSpec((features, width), lambda s, at: (0, s)),
                pl.BlockSpec((width, features), lambda s, at: (s, 0)),
            ],
            out_specs=[
                pl.BlockSpec((1, rows, 3 * width), lambda s, at: (s, 0, 0)),
                pl.BlockSpec((3, chips, 128), lambda s, at: (0, 0, 0)),
            ],
            scratch_shapes=[pltpu.VMEM((2, 2, rows, features), BF16)],
        ),
        compiler_params=pltpu.CompilerParams(vmem_limit_bytes=LIMIT),
    )(at, counts, tok, cot, wg, wu, wd, wg2, wu2, wd2)


def ring_kernel(
    chips, part, table, shares, values, got, stage, bounds, bounds_in, rsend, rrecv, gsend, grecv, vsend, vrecv, tsend, trecv
):
    dp = lax.axis_index("dp")
    core = lax.rem(dp, 2)
    me = (dp - core) // 2
    depth = chips // 2
    half = SUBS // 2
    width = part.shape[3] // 3
    rows = part.shape[2]

    def chip(offset):
        return lax.rem(me + offset + 2 * chips, chips)

    way = [{"dp": 2 * chip(1) + core}, {"dp": 2 * chip(-1) + core}]
    sign = (1, -1)
    greet(way)

    def halves(direction):
        return range(half) if direction == 0 else range(half, SUBS)

    copies = []

    def bound(ref, chunk):
        lines = [jnp.broadcast_to(ref[index, pl.ds(chunk, 1), :], (1, 128)) for index in range(3)]
        return jnp.concatenate([line for line in lines for _ in range(width // 128)], axis=1)

    def reduce_send(direction, step, sub, total, chunk):
        at = (direction, step, sub)
        limit = bound(bounds.at[direction, step], chunk)
        inverse = jnp.where(limit > 1e-30, STEPS / jnp.maximum(limit, 1e-30), 0.0)
        stage[at] = jnp.round(total * inverse).astype(jnp.int32).astype(jnp.int16)
        copies.append(push(stage.at[at], got.at[at], rsend.at[at], rrecv.at[at], way[direction]))

    def reduce_wait(direction, step, sub, chunk):
        at = (direction, step, sub)
        pltpu.make_async_copy(got.at[at], got.at[at], rrecv.at[at]).wait()
        limit = bound(bounds_in.at[direction, step], chunk)
        return got[at].astype(jnp.int32).astype(F32) * (limit * (1.0 / STEPS))

    def bound_send(direction, step):
        at = (direction, step)
        copies.append(push(bounds.at[at], bounds_in.at[at], tsend.at[at], trecv.at[at], way[direction]))

    def bound_wait(direction, step):
        at = (direction, step)
        pltpu.make_async_copy(bounds_in.at[at], bounds_in.at[at], trecv.at[at]).wait()

    for direction in range(2):
        bounds[direction, 0] = table[...]
        bound_send(direction, 0)
    for index in range(half):
        for direction in range(2):
            sub = halves(direction)[index]
            chunk = chip(sign[direction] * depth)
            reduce_send(direction, 0, sub, part[sub, chunk], chunk)
    for step in range(1, depth):
        for direction in range(2):
            bound_wait(direction, step - 1)
            bounds[direction, step] = table[...] + bounds_in[direction, step - 1]
            bound_send(direction, step)
        for index in range(half):
            for direction in range(2):
                if step == 1:
                    sub = halves(1 - direction)[index]
                    chunk = chip(sign[direction] * (depth - 1))
                    reduce_send(direction, 1, sub, part[sub, chunk], chunk)
        for sub in range(SUBS):
            for direction in range(2):
                if step == 1 and sub not in halves(direction):
                    continue
                chunk = chip(sign[direction] * (depth - step))
                total = part[sub, chunk] + reduce_wait(direction, step - 1, sub, chunk)
                reduce_send(direction, step, sub, total, chunk)
    for direction in range(2):
        bound_wait(direction, depth - 1)

    def gather_send(direction, step, sub):
        chunk = shares.at[sub, chip(-sign[direction] * step)]
        at = (direction, step, sub)
        copies.append(push(chunk, chunk, gsend.at[at], grecv.at[at], way[direction]))

    def gather_wait(direction, step, sub):
        chunk = shares.at[sub, chip(-sign[direction] * (step + 1))]
        pltpu.make_async_copy(chunk, chunk, grecv.at[direction, step, sub]).wait()

    def value_send(direction, step):
        chunk = values.at[chip(-sign[direction] * step)]
        at = (direction, step)
        copies.append(push(chunk, chunk, vsend.at[at], vrecv.at[at], way[direction]))

    def value_wait(direction, step):
        chunk = values.at[chip(-sign[direction] * (step + 1))]
        pltpu.make_async_copy(chunk, chunk, vrecv.at[direction, step]).wait()

    inner = jnp.zeros((rows, 1), F32)
    for index in range(half):
        for sub in (halves(0)[index], halves(1)[index]):
            total = part[sub, me]
            for direction in range(2):
                if depth > 1 or sub in halves(direction):
                    total = total + reduce_wait(direction, depth - 1, sub, me)
            gate, up, back = total[:, :width], total[:, width : 2 * width], total[:, 2 * width :]
            logistic = 1.0 / (1.0 + jnp.exp(-gate))
            active = gate * logistic
            hidden = (active * up).astype(BF16)
            shares[sub, me, :, :width] = hidden
            d_gate = back * up * logistic * (1.0 + gate * (1.0 - logistic))
            shares[sub, me, :, width : 2 * width] = d_gate.astype(BF16)
            shares[sub, me, :, 2 * width :] = (back * active).astype(BF16)
            for direction in range(2):
                if depth > 1 or sub in halves(direction):
                    gather_send(direction, 0, sub)
            inner = inner + jnp.sum(hidden.astype(F32) * back, axis=1, keepdims=True)
    lanes = lax.broadcasted_iota(jnp.int32, (rows, 128), 1)
    diagonal = lax.broadcasted_iota(jnp.int32, (rows, 128), 0) == lanes
    line = jnp.sum(jnp.where(diagonal, inner, 0.0), axis=0, keepdims=True)
    values[me] = jnp.broadcast_to(line, (8, 128))
    for direction in range(2):
        if depth > 1 or direction == 0:
            value_send(direction, 0)
    for step in range(1, depth + 1):
        last = step == depth
        for index in range(half):
            for sub in (halves(0)[index], halves(1)[index]):
                for direction in range(2):
                    if last and sub not in halves(direction):
                        continue
                    gather_wait(direction, step - 1, sub)
                    if not last and (step < depth - 1 or sub in halves(direction)):
                        gather_send(direction, step, sub)
        for direction in range(2):
            if last and direction == 1:
                continue
            value_wait(direction, step - 1)
            if not last and (step < depth - 1 or direction == 0):
                value_send(direction, step)
    for copy in copies:
        copy.wait_send()


def ring(chips, ident, part, table):
    _, _, rows, wide = part.shape
    depth = chips // 2
    return pl.pallas_call(
        functools.partial(ring_kernel, chips),
        out_shape=[jax.ShapeDtypeStruct(part.shape, BF16), jax.ShapeDtypeStruct((chips, 8, 128), F32)],
        in_specs=[VMEM] * 2,
        out_specs=[VMEM] * 2,
        scratch_shapes=[pltpu.VMEM((2, depth, SUBS, rows, wide), jnp.int16)] * 2
        + [pltpu.VMEM((2, depth) + table.shape, F32)] * 2
        + [pltpu.SemaphoreType.DMA((2, depth, SUBS))] * 4
        + [pltpu.SemaphoreType.DMA((2, depth))] * 4,
        compiler_params=pltpu.CompilerParams(collective_id=ident, has_side_effects=True, vmem_limit_bytes=LIMIT),
    )(part, table)


def second_kernel(nodes, locals_, at, counts, shares, values, wg, wu, wd, wg2, wu2, wd2, forward_out, back_out, values_out):
    features = wg2.shape[0]
    width = wg2.shape[1] // SUBS
    rows = shares.shape[1]
    slots = forward_out.shape[1]
    own = counts[:, pl.ds(at[1], 1), :].reshape(locals_, 128)
    place = places(nodes, locals_, own)
    row = lax.broadcasted_iota(jnp.int32, (slots, rows), 1).astype(F32)
    unpack = [jnp.where(row == upright(one, slots), 1.0, 0.0).astype(BF16) for one in place]
    for side, (gate, up, down) in enumerate(((wg.at[0], wu.at[0], wd.at[0]), (wg2, wu2, wd2))):
        forward = jnp.zeros((rows, features), F32)
        back = forward
        for sub in range(SUBS):
            units = slice(sub * width, (sub + 1) * width)
            forward = forward + jnp.dot(shares[sub, :, :width], down[units, :], preferred_element_type=F32)
            back = back + lax.dot_general(
                shares[sub, :, width : 2 * width], gate[:, units], NT, preferred_element_type=F32
            )
            back = back + lax.dot_general(shares[sub, :, 2 * width :], up[:, units], NT, preferred_element_type=F32)
        for matrix, value, out in ((unpack[0], forward, forward_out), (unpack[1], back, back_out)):
            out[side] = jnp.dot(matrix, value.astype(BF16), preferred_element_type=F32).astype(BF16)
    chips = values.shape[0]
    share = rows // chips
    value = jnp.concatenate([upright(values[chip, 0:1, :], share) for chip in range(chips)], axis=0)
    row = lax.broadcasted_iota(jnp.int32, (rows, slots), 0).astype(F32)
    value = jnp.sum(jnp.where(row == place[0], value, 0.0), axis=0, keepdims=True)
    values_out[...] = jnp.zeros_like(values_out)
    part = slots // locals_
    for relay in range(locals_):
        values_out[relay, :, :part] = jnp.broadcast_to(value[:, relay * part : (relay + 1) * part], (8, part))


def second(nodes, locals_, at, counts, shares, values, wg, wu, wd, wg2, wu2, wd2):
    _, rows, wide = shares.shape
    features, hidden = wg2.shape
    slots = nodes * locals_ * CAP
    side = pl.BlockSpec((features, hidden), lambda i, at: (0, 0))
    out = jax.ShapeDtypeStruct((2, slots, features), BF16)
    return pl.pallas_call(
        functools.partial(second_kernel, nodes, locals_),
        out_shape=[out, out, jax.ShapeDtypeStruct((locals_, 8, 128), F32)],
        grid_spec=pltpu.PrefetchScalarGridSpec(
            num_scalar_prefetch=1,
            grid=(1,),
            in_specs=[
                pl.BlockSpec(counts.shape, lambda i, at: (0, 0, 0)),
                pl.BlockSpec((SUBS, rows, wide), lambda i, at: (0, 0, 0)),
                pl.BlockSpec(values.shape, lambda i, at: (0, 0, 0)),
                pl.BlockSpec((1, features, hidden), lambda i, at: (at[0], 0, 0)),
                pl.BlockSpec((1, features, hidden), lambda i, at: (at[0], 0, 0)),
                pl.BlockSpec((1, hidden, features), lambda i, at: (at[0], 0, 0)),
                side,
                side,
                pl.BlockSpec((hidden, features), lambda i, at: (0, 0)),
            ],
            out_specs=[
                pl.BlockSpec((2, slots, features), lambda i, at: (0, 0, 0)),
                pl.BlockSpec((2, slots, features), lambda i, at: (0, 0, 0)),
                pl.BlockSpec((locals_, 8, 128), lambda i, at: (0, 0, 0)),
            ],
        ),
        compiler_params=pltpu.CompilerParams(vmem_limit_bytes=LIMIT),
    )(at, counts, shares, values, wg, wu, wd, wg2, wu2, wd2)


def return_kernel(nodes, locals_, forward, back, values, forward_in, back_in, values_in, send, recv, vsend, vrecv):
    core, ways, everyone = paths_of(nodes, locals_)
    greet(everyone)
    copies = []
    for step in list(range(1, max(nodes, locals_))) + [0]:
        for path, ((me, at, same, cross), src, dst) in enumerate(zip(ways, (forward, back), (forward_in, back_in))):
            mine = 2 * me + core
            for far, peers in enumerate((same, cross)):
                if step >= len(at) or (step == 0 and far == 0):
                    continue
                sem = (path, step, far)
                copies.append(push(src.at[far, at[step]], dst.at[mine], send.at[sem], recv.at[sem], peers[step]))
                if path == 0:
                    sem = (step, far)
                    line = values.at[at[step]]
                    copies.append(push(line, values_in.at[mine], vsend.at[sem], vrecv.at[sem], peers[step]))
    for (me, _, _, _), src, dst in zip(ways, (forward, back), (forward_in, back_in)):
        dst[2 * me + core] = src[0, me]
    me = ways[0][0]
    values_in[2 * me + core] = values[me]
    for copy in copies:
        copy.wait()


def give_back(nodes, locals_, forward, back, values):
    most = max(nodes, locals_)
    return pl.pallas_call(
        functools.partial(return_kernel, nodes, locals_),
        out_shape=[
            jax.ShapeDtypeStruct((2 * locals_,) + forward.shape[2:], BF16),
            jax.ShapeDtypeStruct((2 * nodes,) + back.shape[2:], BF16),
            jax.ShapeDtypeStruct((2 * locals_, 8, 128), F32),
        ],
        in_specs=[VMEM] * 3,
        out_specs=[VMEM] * 3,
        scratch_shapes=[pltpu.SemaphoreType.DMA((2, most, 2))] * 2 + [pltpu.SemaphoreType.DMA((locals_, 2))] * 2,
        compiler_params=pltpu.CompilerParams(collective_id=3, has_side_effects=True, vmem_limit_bytes=LIMIT),
    )(forward, back, values)


def combine_kernel(top, nodes, locals_, scale, metaz, metal, forward, back, vback, count, forward_out, back_out, gates_out):
    rows = forward_out.shape[1]
    for path, (meta, src, out) in enumerate(((metaz, forward, forward_out), (metal, back, back_out))):
        experts, slots, wide = src.shape
        weights, routes = lay_out(meta, top, rows)
        columns = routes.shape[1]
        name, _, code = slot_codes(rows, top, routes, names_of(path, nodes, locals_))
        weight = jnp.zeros((experts, columns), F32)
        for k in range(top):
            weight = weight + jnp.where(routes[k : k + 1, :] == name, weights[k : k + 1, :], 0.0)
        place = lax.broadcasted_iota(jnp.int32, (1, slots, 1), 1).astype(F32)
        hit = code[:, None, :] == place
        rows_back = src[...].reshape(experts * slots, wide)
        high = weight.astype(BF16).astype(F32)
        total = jnp.zeros((columns, wide), F32)
        for share in (high, weight - high):
            spread_ = jnp.where(hit, share[:, None, :], 0.0).astype(BF16).reshape(experts * slots, columns)
            total = total + lax.dot_general(spread_, rows_back, (((0,), (0,)), ((), ())), preferred_element_type=F32)
        out[...] = total.astype(BF16).reshape(out.shape)
        if path == 0:
            lanes = lax.broadcasted_iota(jnp.int32, (experts, slots, 128), 2)
            diagonal = lax.broadcasted_iota(jnp.int32, (experts, slots, 128), 1) == lanes
            value = jnp.sum(jnp.where(diagonal, vback[:, 0:1, :], 0.0), axis=2, keepdims=True)
            inner = jnp.sum(jnp.where(hit, value, 0.0), axis=1)
            number = jnp.sum(count[:experts, :], axis=1, keepdims=True)
            inner = inner + BALANCE * scale * number
            gates = [
                jnp.sum(jnp.where(routes[k : k + 1, :] == name, inner, 0.0), axis=0, keepdims=True)
                for k in range(top)
            ]
            gates = jnp.concatenate(gates, axis=0)
            gates_out[...] = jnp.zeros_like(gates_out)
            for i in range(nodes):
                gates_out[i, :, :rows] = gates[:, i * rows : (i + 1) * rows]


def combine(top, nodes, locals_, scale, rows, metaz, metal, forward, back, vback, count):
    return pl.pallas_call(
        functools.partial(combine_kernel, top, nodes, locals_, scale),
        out_shape=[
            jax.ShapeDtypeStruct((nodes, rows, forward.shape[2]), BF16),
            jax.ShapeDtypeStruct((locals_, rows, back.shape[2]), BF16),
            jax.ShapeDtypeStruct((nodes, top, 128), F32),
        ],
        in_specs=[VMEM] * 6,
        out_specs=[VMEM] * 3,
        compiler_params=pltpu.CompilerParams(vmem_limit_bytes=LIMIT),
    )(metaz, metal, forward, back, vback, count)


def home_kernel(nodes, locals_, forward, back, gates, forward_in, back_in, gates_in, send, recv):
    node, nodes_at = ring_of("node", nodes)
    place, locals_at = ring_of("local", locals_)
    far = [{"node": at} for at in nodes_at]
    side = [{"local": at} for at in locals_at]
    greet(far[1:] + side[1:])
    copies = []
    for step in range(1, max(nodes, locals_)):
        for index, (src, dst, at, peers) in enumerate(
            (
                (gates, gates_in, nodes_at, far),
                (forward, forward_in, nodes_at, far),
                (back, back_in, locals_at, side),
            )
        ):
            if step < len(peers):
                sem = (step - 1, index)
                copies.append(push(src.at[at[step]], dst.at[step], send.at[sem], recv.at[sem], peers[step]))
    for src, dst, me in ((gates, gates_in, node), (forward, forward_in, node), (back, back_in, place)):
        dst[0] = src[me]
    for copy in copies:
        copy.wait()


def home(nodes, locals_, forward, back, gates):
    most = max(nodes, locals_) - 1
    return pl.pallas_call(
        functools.partial(home_kernel, nodes, locals_),
        out_shape=[jax.ShapeDtypeStruct(a.shape, a.dtype) for a in (forward, back, gates)],
        in_specs=[VMEM] * 3,
        out_specs=[VMEM] * 3,
        scratch_shapes=[pltpu.SemaphoreType.DMA((most, 3))] * 2,
        compiler_params=pltpu.CompilerParams(collective_id=4, has_side_effects=True, vmem_limit_bytes=LIMIT),
    )(forward, back, gates)


def total_kernel(forward, back, gates, mixed, grads, gates_out):
    mixed[...] = jnp.sum(forward[...].astype(F32), axis=0).astype(BF16)
    grads[...] = jnp.sum(back[...].astype(F32), axis=0).astype(BF16)
    gate = jnp.sum(gates[...], axis=0)
    for k in range(gates_out.shape[1]):
        gates_out[:, k : k + 1] = upright(gate[k : k + 1, :], gates_out.shape[0])


def total(forward, back, gates):
    _, rows, features = forward.shape
    half = jax.ShapeDtypeStruct((rows, features), BF16)
    return pl.pallas_call(
        total_kernel,
        out_shape=[half, half, jax.ShapeDtypeStruct((rows, gates.shape[1]), F32)],
        in_specs=[VMEM] * 3,
        out_specs=[VMEM] * 3,
        compiler_params=pltpu.CompilerParams(vmem_limit_bytes=LIMIT),
    )(forward, back, gates)


def middle(chips, nodes, locals_, rows, ident, at, counts, tok, cot, *weights):
    part, table = first(chips, nodes, locals_, rows, at, counts, tok, cot, *weights)
    shares, values = ring(chips, ident, part.reshape(SUBS, chips, rows // chips, part.shape[2]), table)
    return second(nodes, locals_, at, counts, shares.reshape(part.shape), values, *weights)


def body(chips, nodes, locals_, tokens, cotangent, routes, gate_weights, w_gate, w_up, w_down):
    rows, features = tokens.shape
    top = routes.shape[1]
    slots = nodes * locals_ * CAP
    core = lax.rem(lax.axis_index("dp"), 2)
    at = jnp.stack([core, 2 * lax.axis_index("local") + core]).astype(jnp.int32)
    tokz, cotl, metaz, metal, *swapped = spread(
        nodes, locals_, tokens, cotangent, gate_weights, routes, w_gate, w_up, w_down
    )
    tok, cot, count = select(top, nodes, locals_, tokz, cotl, metaz, metal)
    tok, cot, counts, count_sum = slots_exchange(nodes, locals_, tok, cot, count)
    inputs = (
        at, counts, tok.reshape(2, slots, features), cot.reshape(2, slots, features), w_gate, w_up, w_down, *swapped
    )
    usual = functools.partial(middle, chips, nodes, locals_, USUAL * chips, 2)
    every = functools.partial(middle, chips, nodes, locals_, slots, 5)
    crowded = jnp.max(count_sum[2 * locals_ :, :]) > USUAL * chips
    forward, back, values = lax.cond(crowded, every, usual, *inputs)
    forward = forward.reshape(2, locals_, nodes * CAP, features)
    back = back.reshape(2, nodes, locals_ * CAP, features)
    forward, back, values = give_back(nodes, locals_, forward, back, values)
    scale = 2 * nodes * locals_ / (top * rows * nodes * locals_)
    summed = combine(top, nodes, locals_, scale, rows, metaz, metal, forward, back, values, count_sum)
    return total(*home(nodes, locals_, *summed))


def solution(mesh):
    chips, nodes, locals_ = mesh.shape["dp"] // 2, mesh.shape["node"], mesh.shape["local"]
    placed = (
        P(("node", "local"), "dp"),
        P(("node", "local"), "dp"),
        P(("node", "local"), None),
        P(("node", "local"), None),
        P(("node", "local"), "dp", None),
        P(("node", "local"), "dp", None),
        P(("node", "local"), None, "dp"),
    )
    return jax.shard_map(
        functools.partial(body, chips, nodes, locals_),
        mesh=mesh,
        in_specs=placed,
        out_specs=(
            P(("node", "local"), "dp"),
            P(("node", "local"), "dp"),
            P(("node", "local"), None),
        ),
        check_vma=False,
    )
```

time: 189 us -> 158 us (0.84)
  Pallas kernels: 181 us -> 149 us
    pallas_call x8 -> x9, Pallas kernels: 126 us -> 109 us  [the longest x1 29.2 us: spread(): pl.pallas_call(functools.partial(spread_kernel, nodes, locals_), out_shap...]
    pallas_call x1, Pallas kernels: 54.6 us -> 40.3 us  [ring(): pl.pallas_call(functools.partial(ring_kernel, chips), out_shape=[jax.Shap...]
where the time goes in v2:
time: 158 us; the launch traced here: 157 us
  Pallas kernels  149 us (94%)
  local copies, waits for them, and re-layouts  4.33 us (3%)
    pallas_call x1, Pallas kernels, ring(): pl.pallas_call(functools.partial(ring_kernel, chips), out_shape=[jax.Shap...  40.3 us
    pallas_call x1, Pallas kernels, spread(): pl.pallas_call(functools.partial(spread_kernel, nodes, locals_), out_shap...  29.2 us
    pallas_call x1, Pallas kernels, give_back(): pl.pallas_call(functools.partial(return_kernel, nodes, locals_), out_shap...  24.3 us
    pallas_call x1, Pallas kernels, slots_exchange(): pl.pallas_call(functools.partial(slots_kernel, nodes, locals_), out_shape...  23.4 us
    pallas_call x1, Pallas kernels, home(): pl.pallas_call(functools.partial(home_kernel, nodes, locals_), out_shape=...  13.8 us
    pallas_call x1, Pallas kernels, first(): pl.pallas_call(functools.partial(first_kernel, chips, nodes, locals_), ou...  6.2 us
    pallas_call x1, Pallas kernels, second(): pl.pallas_call(functools.partial(second_kernel, nodes, locals_), out_shap...  3.89 us
    pallas_call x1, Pallas kernels, combine(): pl.pallas_call(functools.partial(combine_kernel, top, nodes, locals_, sca...  3.77 us

profile of v2, /device:TPU:1, one launch (start us, length us, event | category | flops | bytes accessed | tf_op | source)
XLA Modules:
  0.0 156.8 jit_solution(13326068784669118531)
XLA Ops:
  0.6 0.0 copy-start.2
  0.6 0.0 copy-start.1
  0.7 0.0 copy-start
  0.7 0.1 pad_add_fusion
  0.7 1.5 copy.11.routes
  2.3 1.4 copy.10.gates
  3.6 29.2 %shard_map.94 = (bf16[8,48,256]{2,1,0:T(8,128)(2,1)}, bf16[8,48,256]{2,1,0:T(8,128)(2,1)}, f32[8,16,128]{2,1,0:T(8,128)}, f32[8,16,128]{2,1,0:T(8,128)}, bf16[25...) custom-call(bf16[48,256]{1,0:T(8,128)(2,1)} %tok.1, bf16[48,256]{1,0:T(8,128)(2,1)} %cot.1, ...), custom_call_target="tpu_custom_call" | custom-call | tf_op jit(solution)/shard_map/pallas_call | solution.py:96
  32.9 2.8 %shard_map.95 = (bf16[16,48,256]{2,1,0:T(8,128)(2,1)}, bf16[16,48,256]{2,1,0:T(8,128)(2,1)}, f32[24,128]{1,0:T(8,128)}) custom-call(bf16[8,48,256]{2,1,0:T(8,128)(2,1)} %get-tuple-element.117.tokz, bf16[8,48,256]{2,1,0:T(8,128)(2,1)} %get-tuple-element.118.cotl, f32[8,16,128]{2,1,0:T(8,128)} %get-tuple-element.115.metaz, f32[8,16,128]{2,1,0:T(8,128)} %get-tuple-element.116.metal), custom_call_target="tpu_custom_call" | custom-call | tf_op jit(solution)/shard_map/pallas_call | solution.py:172
  35.7 23.4 %shard_map.96 = (bf16[2,8,48,256]{3,2,1,0:T(8,128)(2,1)S(1)}, bf16[2,8,48,256]{3,2,1,0:T(8,128)(2,1)}, f32[8,24,128]{2,1,0:T(8,128)}, f32[24,128]{1,0:T(8,128)}) custom-call(bf16[16,48,256]{2,1,0:T(8,128)(2,1)} %get-tuple-element.119.tok, bf16[16,48,256]{2,1,0:T(8,128)(2,1)} %get-tuple-element.120.cot, f32[24,128]{1,0:T(8,128)} %get-tuple-element.121.count), custom_call_target="tpu_custom_call" | custom-call | tf_op jit(solution)/shard_map/pallas_call | solution.py:221
  59.1 1.3 slice_reduce_fusion
  61.1 0.0 copy-done.2
  61.1 0.0 copy-done.1
  61.1 0.0 copy-done
  61.1 50.7 %conditional.1 = (f32[8,8,128]{2,1,0:T(8,128)S(1)}, bf16[2,8,48,256]{3,2,1,0:T(8,128)(2,1)S(1)}, bf16[2,8,48,256]{3,2,1,0:T(8,128)(2,1)S(1)}) conditional(s32[]{:T(128)} %convert_element_type.3, (bf16[2,8,48,256]{3,2,1,0:T(8,128)(2,1)S(1)}, bf16[2,8,48,256]{3,2,1,0:T(8,128)(2,1)}, s32[2]{0:T(128)S(1)}, f32[8,24,128]{2,1,0:T(8,128)}, ...), branch_computations={%region_1.0_spmd, %region_2.0_spmd} | conditional | bytes 6684808 | solution.py:718
  61.1 0.0 copy-start.3
  61.1 0.0 copy-start.5
  61.1 0.0 copy-start.7
  61.1 0.0 copy-start.9
  61.2 6.2 %branch_0_fun.3 = (f32[4,256,768]{2,1,0:T(8,128)}, f32[3,8,128]{2,1,0:T(8,128)}) custom-call(s32[2]{0:T(128)S(1)} %get-tuple-element.52.at, f32[8,24,128]{2,1,0:T(8,128)} %get-tuple-element.53.counts, bf16[2,384,256]{2,1,0:T(8,128)(2,1)S(1)} %bitcast.17, bf16[2,384,256]{2,1,0:T(8,128)(2,1)} %bitcast.19, bf16[2,256,1024]{2,1,0:T(8,128)(2,1)S(1)} %get-tuple-element.56.wg, ...), custom_call_target="tpu_custom_call" | custom-call | tf_op jit(solution)/shard_map/cond/branch_0_fun/pallas_call | solution.py:297
  67.3 40.3 %branch_0_fun.4 = (bf16[4,8,32,768]{3,2,1,0:T(8,128)(2,1)}, f32[8,8,128]{2,1,0:T(8,128)}) custom-call(f32[4,8,32,768]{3,2,1,0:T(8,128)} %bitcast.15, f32[3,8,128]{2,1,0:T(8,128)} %get-tuple-element.63.table), custom_call_target="tpu_custom_call" | custom-call | tf_op jit(solution)/shard_map/cond/branch_0_fun/pallas_call | solution.py:471
  107.6 0.0 copy-done.3
  107.7 0.0 copy-done.5
  107.7 0.0 copy-done.7
  107.7 0.0 copy-done.9
  107.7 3.9 %branch_0_fun.5 = (bf16[2,384,256]{2,1,0:T(8,128)(2,1)S(1)}, bf16[2,384,256]{2,1,0:T(8,128)(2,1)S(1)}, f32[8,8,128]{2,1,0:T(8,128)S(1)}) custom-call(s32[2]{0:T(128)S(1)} %get-tuple-element.52.at, f32[8,24,128]{2,1,0:T(8,128)S(1)} %copy-done.9, bf16[4,256,768]{2,1,0:T(8,128)(2,1)} %bitcast.21, f32[8,8,128]{2,1,0:T(8,128)} %get-tuple-element.65.values, ...), custom_call_target="tpu_custom_call" | custom-call | tf_op jit(solution)/shard_map/cond/branch_0_fun/pallas_call | solution.py:522
  111.8 24.3 %shard_map.97 = (bf16[16,48,256]{2,1,0:T(8,128)(2,1)}, bf16[16,48,256]{2,1,0:T(8,128)(2,1)}, f32[16,8,128]{2,1,0:T(8,128)}) custom-call(bf16[2,8,48,256]{3,2,1,0:T(8,128)(2,1)S(1)} %get-tuple-element.129.forward, bf16[2,8,48,256]{3,2,1,0:T(8,128)(2,1)S(1)} %get-tuple-element.130.back, f32[8,8,128]{2,1,0:T(8,128)S(1)} %get-tuple-element.131.values), custom_call_target="tpu_custom_call" | custom-call | tf_op jit(solution)/shard_map/pallas_call | solution.py:575
  136.1 3.8 %shard_map.98 = (bf16[8,48,256]{2,1,0:T(8,128)(2,1)}, bf16[8,48,256]{2,1,0:T(8,128)(2,1)}, f32[8,8,128]{2,1,0:T(8,128)}) custom-call(f32[8,16,128]{2,1,0:T(8,128)} %get-tuple-element.115.metaz, f32[8,16,128]{2,1,0:T(8,128)} %get-tuple-element.116.metal, bf16[16,48,256]{2,1,0:T(8,128)(2,1)} %get-tuple-element.132.forward, ...), custom_call_target="tpu_custom_call" | custom-call | tf_op jit(solution)/shard_map/pallas_call | solution.py:626
  139.8 13.8 %shard_map.99 = (bf16[8,48,256]{2,1,0:T(8,128)(2,1)}, bf16[8,48,256]{2,1,0:T(8,128)(2,1)}, f32[8,8,128]{2,1,0:T(8,128)}) custom-call(bf16[8,48,256]{2,1,0:T(8,128)(2,1)} %get-tuple-element.135.forward, bf16[8,48,256]{2,1,0:T(8,128)(2,1)} %get-tuple-element.136.back, f32[8,8,128]{2,1,0:T(8,128)} %get-tuple-element.137.gates), custom_call_target="tpu_custom_call" | custom-call | tf_op jit(solution)/shard_map/pallas_call | solution.py:665
  153.7 1.8 %shard_map.100 = (bf16[48,256]{1,0:T(8,128)(2,1)}, bf16[48,256]{1,0:T(8,128)(2,1)}, f32[48,8]{1,0:T(8,128)}) custom-call(bf16[8,48,256]{2,1,0:T(8,128)(2,1)} %get-tuple-element.138.forward, bf16[8,48,256]{2,1,0:T(8,128)(2,1)} %get-tuple-element.139.back, f32[8,8,128]{2,1,0:T(8,128)} %get-tuple-element.140.gates), custom_call_target="tpu_custom_call" | custom-call | tf_op jit(solution)/shard_map/pallas_call | solution.py:686
  155.4 1.4 copy.12
Async XLA Ops:
  0.6 60.4 %copy-start.2 = (bf16[2,1024,256]{2,1,0:T(8,128)(2,1)S(1)}, bf16[2,1024,256]{2,1,0:T(8,128)(2,1)}, u32[]{:S(2)}) copy-start(bf16[2,1024,256]{2,1,0:T(8,128)(2,1)} %wd.1) | copy-start | bytes 3145732
  0.6 60.4 %copy-start.1 = (bf16[2,256,1024]{2,1,0:T(8,128)(2,1)S(1)}, bf16[2,256,1024]{2,1,0:T(8,128)(2,1)}, u32[]{:S(2)}) copy-start(bf16[2,256,1024]{2,1,0:T(8,128)(2,1)} %wu.1) | copy-start | bytes 3145732
  0.7 60.4 %copy-start = (bf16[2,256,1024]{2,1,0:T(8,128)(2,1)S(1)}, bf16[2,256,1024]{2,1,0:T(8,128)(2,1)}, u32[]{:S(2)}) copy-start(bf16[2,256,1024]{2,1,0:T(8,128)(2,1)} %wg.1) | copy-start | bytes 3145732
  61.1 46.5 %copy-start.3 = (bf16[256,1024]{1,0:T(8,128)(2,1)S(1)}, bf16[256,1024]{1,0:T(8,128)(2,1)}, u32[]{:S(2)}) copy-start(bf16[256,1024]{1,0:T(8,128)(2,1)} %get-tuple-element.59.wg2) | copy-start | bytes 1572868 | tf_op jit(solution)/shard_map/cond
  61.1 46.5 %copy-start.5 = (bf16[256,1024]{1,0:T(8,128)(2,1)S(1)}, bf16[256,1024]{1,0:T(8,128)(2,1)}, u32[]{:S(2)}) copy-start(bf16[256,1024]{1,0:T(8,128)(2,1)} %get-tuple-element.60.wu2) | copy-start | bytes 1572868 | tf_op jit(solution)/shard_map/cond
  61.1 46.5 %copy-start.7 = (bf16[1024,256]{1,0:T(8,128)(2,1)S(1)}, bf16[1024,256]{1,0:T(8,128)(2,1)}, u32[]{:S(2)}) copy-start(bf16[1024,256]{1,0:T(8,128)(2,1)} %get-tuple-element.61.wd2) | copy-start | bytes 1572868 | tf_op jit(solution)/shard_map/cond
  61.1 46.5 %copy-start.9 = (f32[8,24,128]{2,1,0:T(8,128)S(1)}, f32[8,24,128]{2,1,0:T(8,128)}, u32[]{:S(2)}) copy-start(f32[8,24,128]{2,1,0:T(8,128)} %get-tuple-element.53.counts) | copy-start | bytes 294916 | tf_op jit(solution)/shard_map/cond

commit v3 on v0

v3 whole, which is shorter than its diff:
```python
import functools

import jax
import jax.numpy as jnp
from jax import lax
from jax.experimental import pallas as pl
from jax.experimental.pallas import tpu as pltpu
from jax.sharding import PartitionSpec as P

BALANCE = 2.0
CAP = 6
USUAL = 32
SUBS = 4
STEPS = 32766.0
MESH = pl.DeviceIdType.MESH
F32, BF16 = jnp.float32, jnp.bfloat16
VMEM = pl.BlockSpec(memory_space=pltpu.VMEM)
ANY = pl.BlockSpec(memory_space=pl.ANY)
LIMIT = 56 * 1024 * 1024


def greet(peers):
    barrier = pltpu.get_barrier_semaphore()
    for peer in peers:
        pl.semaphore_signal(barrier, inc=1, device_id=peer, device_id_type=MESH)
    pl.semaphore_wait(barrier, len(peers))


def push(src, dst, send, recv, peer):
    copy = pltpu.make_async_remote_copy(
        src_ref=src, dst_ref=dst, send_sem=send, recv_sem=recv, device_id=peer, device_id_type=MESH
    )
    copy.start()
    return copy


def other_core():
    core = lax.rem(lax.axis_index("dp"), 2)
    return core, lax.axis_index("dp") + 1 - 2 * core


def upright(line, rows):
    lanes = lax.broadcasted_iota(jnp.int32, (rows, line.shape[-1]), 1)
    diagonal = lax.broadcasted_iota(jnp.int32, (rows, line.shape[-1]), 0) == lanes
    return jnp.sum(jnp.where(diagonal, line, 0.0), axis=1, keepdims=True)


def lying(column, lanes):
    rows = column.shape[0]
    lane = lax.broadcasted_iota(jnp.int32, (rows, lanes), 1)
    diagonal = lax.broadcasted_iota(jnp.int32, (rows, lanes), 0) == lane
    return jnp.sum(jnp.where(diagonal, column, 0.0), axis=0, keepdims=True)


def ring_of(axis, size):
    me = lax.axis_index(axis)
    return me, [lax.rem(me + step, size) for step in range(size)]


def names_of(path, nodes, locals_):
    if path == 0:
        return lax.broadcasted_iota(jnp.int32, (2 * locals_, 1), 0) + 2 * locals_ * lax.axis_index("node")
    order = lax.broadcasted_iota(jnp.int32, (2 * nodes, 1), 0)
    return (order >> 1) * (2 * locals_) + (order & 1) + 2 * lax.axis_index("local")


def slot_codes(rows, top, routes, names):
    columns = routes.shape[1]
    experts = names.shape[0]
    name = jnp.broadcast_to(names.astype(F32), (experts, columns))
    chosen = jnp.zeros((experts, columns), F32)
    for k in range(top):
        chosen = chosen + jnp.where(routes[k : k + 1, :] == name, 1.0, 0.0)
    scale = -(-32768 // rows)
    earlier = lax.broadcasted_iota(jnp.int32, (columns, columns), 0)
    later = lax.broadcasted_iota(jnp.int32, (columns, columns), 1)
    block_row = (earlier * scale) >> 15
    block_col = (later * scale) >> 15
    before = jnp.where((block_row == block_col) & (earlier < later), 1.0, 0.0).astype(BF16)
    rank = jnp.dot(chosen.astype(BF16), before, preferred_element_type=F32)
    block = (lax.broadcasted_iota(jnp.int32, (experts, columns), 1) * scale >> 15).astype(F32)
    code = jnp.where(chosen > 0.0, block * CAP + rank, -1.0)
    return name, chosen, code


def lay_out(meta, top, rows):
    blocks = meta.shape[0]
    weights = jnp.concatenate([meta[i, :top, :rows] for i in range(blocks)], axis=1)
    routes = jnp.concatenate([meta[i, top : 2 * top, :rows] for i in range(blocks)], axis=1)
    return weights, routes


def paths_of(nodes, locals_):
    core, twin = other_core()
    ways = []
    for axis, size in (("local", locals_), ("node", nodes)):
        me, at = ring_of(axis, size)
        ways.append((me, at, [{axis: one} for one in at], [{axis: one, "dp": twin} for one in at]))
    peers = ways[0][2][1:] + ways[1][2][1:] + ways[0][3] + ways[1][3][1:]
    return core, ways, peers


def choose(path, top, nodes, locals_, src, meta, dst, count):
    rows, features = src.shape[1:]
    experts, slots, _ = dst.shape
    _, routes = lay_out(meta, top, rows)
    columns = routes.shape[1]
    _, chosen, code = slot_codes(rows, top, routes, names_of(path, nodes, locals_))
    place = lax.broadcasted_iota(jnp.int32, (1, slots, 1), 1).astype(F32)
    pick = jnp.where(code[:, None, :] == place, 1.0, 0.0).astype(BF16).reshape(experts * slots, columns)
    got = jnp.dot(pick, src[...].reshape(columns, features), preferred_element_type=F32)
    dst[...] = got.astype(BF16).reshape(experts, slots, features)
    if path == 0:
        block = (lax.broadcasted_iota(jnp.int32, (columns, 128), 0) * -(-32768 // rows)) >> 15
        by_block = jnp.where(block == lax.broadcasted_iota(jnp.int32, (columns, 128), 1), 1.0, 0.0).astype(BF16)
        count[:experts, :] = jnp.dot(chosen.astype(BF16), by_block, preferred_element_type=F32)
        total = 2 * nodes * locals_
        name = lax.broadcasted_iota(jnp.int32, (total, columns), 0).astype(F32)
        hits = jnp.zeros((total, columns), F32)
        for k in range(top):
            hits = hits + jnp.where(routes[k : k + 1, :] == name, 1.0, 0.0)
        count[experts:, :] = jnp.broadcast_to(lying(jnp.sum(hits, axis=1, keepdims=True), 128), (8, 128))


def front_kernel(
    nodes, locals_, tok, cot, gates, routes, wg, wu, wd,
    tok_in, cot_in, counts, count_sum, metaz, metal, wg2, wu2, wd2,
    meta, tokz, cotl, tok_out, cot_out, count, send, recv, wsend, wrecv, ssend, srecv, csend, crecv,
):
    node, nodes_at = ring_of("node", nodes)
    place, locals_at = ring_of("local", locals_)
    core, twin = other_core()
    top, rows = gates.shape
    meta[...] = jnp.zeros_like(meta)
    meta[:top, :rows] = gates[...]
    meta[top:, :rows] = routes[...].astype(F32)
    far = [{"node": at} for at in nodes_at]
    side = [{"local": at} for at in locals_at]
    core, ways, everyone = paths_of(nodes, locals_)
    greet(everyone)
    blocks = [[], []]
    for step in range(1, max(nodes, locals_)):
        for path, (peers, me, arrays) in enumerate(
            ((far, node, ((meta, metaz), (tok, tokz))), (side, place, ((meta, metal), (cot, cotl))))
        ):
            if step < len(peers):
                for index, (src, dst) in enumerate(arrays):
                    at = (path, step - 1, index)
                    blocks[path].append(push(src, dst.at[me], send.at[at], recv.at[at], peers[step]))
    tokz[node] = tok[...]
    cotl[place] = cot[...]
    metaz[node] = meta[...]
    metal[place] = meta[...]
    copies = []
    for path, (src, met, out, dst) in enumerate(((tokz, metaz, tok_out, tok_in), (cotl, metal, cot_out, cot_in))):
        for copy in blocks[path]:
            copy.wait_recv()
        choose(path, top, nodes, locals_, src, met, out, count)
        me, at, same, cross = ways[path]
        if path == 0:
            for step in range(1, locals_):
                sem = step - 1
                copies.append(push(count, counts.at[me], csend.at[sem], crecv.at[sem], same[step]))
        for step in list(range(1, len(at))) + [0]:
            for distant, peers in enumerate((same, cross)):
                if step == 0 and distant == 0:
                    continue
                expert = 2 * at[step] + (core if distant == 0 else 1 - core)
                sem = (path, step, distant)
                copies.append(push(out.at[expert], dst.at[distant, me], ssend.at[sem], srecv.at[sem], peers[step]))
        dst[0, me] = out[2 * me + core]
    counts[place] = count[...]
    for index, (src, dst) in enumerate(((wg, wg2), (wu, wu2), (wd, wd2))):
        copies.append(push(src.at[1 - core], dst, wsend.at[index], wrecv.at[index], {"dp": twin}))
    for copy in copies:
        copy.wait()
    for path in range(2):
        for copy in blocks[path]:
            copy.wait_send()
    count_sum[...] = jnp.sum(counts[...], axis=0)


def front(nodes, locals_, tok, cot, gates, routes, wg, wu, wd):
    features = tok.shape[1]
    most = max(nodes, locals_)
    meta = (2 * gates.shape[0], 128)
    count = (2 * locals_ + 8, 128)
    return pl.pallas_call(
        functools.partial(front_kernel, nodes, locals_),
        out_shape=[
            jax.ShapeDtypeStruct((2, locals_, nodes * CAP, features), BF16),
            jax.ShapeDtypeStruct((2, nodes, locals_ * CAP, features), BF16),
            jax.ShapeDtypeStruct((locals_,) + count, F32),
            jax.ShapeDtypeStruct(count, F32),
            jax.ShapeDtypeStruct((nodes,) + meta, F32),
            jax.ShapeDtypeStruct((locals_,) + meta, F32),
        ]
        + [jax.ShapeDtypeStruct(a.shape[1:], a.dtype) for a in (wg, wu, wd)],
        in_specs=[VMEM] * 4 + [ANY] * 3,
        out_specs=[VMEM] * 6 + [ANY] * 3,
        scratch_shapes=[
            pltpu.VMEM(meta, F32),
            pltpu.VMEM((nodes,) + tok.shape, BF16),
            pltpu.VMEM((locals_,) + cot.shape, BF16),
            pltpu.VMEM((2 * locals_, nodes * CAP, features), BF16),
            pltpu.VMEM((2 * nodes, locals_ * CAP, features), BF16),
            pltpu.VMEM(count, F32),
        ]
        + [pltpu.SemaphoreType.DMA((2, most, 2))] * 2
        + [pltpu.SemaphoreType.DMA((3,))] * 2
        + [pltpu.SemaphoreType.DMA((2, most, 2))] * 2
        + [pltpu.SemaphoreType.DMA((locals_,))] * 2,
        compiler_params=pltpu.CompilerParams(collective_id=0, has_side_effects=True, vmem_limit_bytes=LIMIT),
    )(tok, cot, gates, routes, wg, wu, wd)


NT = (((1,), (1,)), ((), ()))


def places(nodes, locals_, counts):
    slots = nodes * locals_ * CAP
    index = lax.broadcasted_iota(jnp.int32, (locals_, slots), 1).astype(F32)
    axis = lax.broadcasted_iota(jnp.int32, (locals_, slots), 0).astype(F32)
    lane = lax.broadcasted_iota(jnp.int32, (128, slots), 0).astype(F32)
    earlier = lax.broadcasted_iota(jnp.int32, (slots, slots), 0).astype(F32)
    rows, valid = [], None
    for path, inner in enumerate((nodes, locals_)):
        major = jnp.floor((index + 0.5) * (1.0 / (CAP * inner)))
        within = index - major * (CAP * inner)
        minor = jnp.floor((within + 0.5) * (1.0 / CAP))
        rank = within - minor * CAP
        of_node, of_local = (minor, major) if path == 0 else (major, minor)
        by_node = jnp.where(lane == of_node[:1, :], 1.0, 0.0).astype(BF16)
        count = jnp.dot(counts.astype(BF16), by_node, preferred_element_type=F32)
        count = jnp.sum(jnp.where(axis == of_local, count, 0.0), axis=0, keepdims=True)
        filled = rank[:1, :] < count
        if path == 0:
            valid = jnp.broadcast_to(jnp.where(filled, 1.0, 0.0), (8, slots)).astype(BF16)
        first_path = of_local[:1, :] * (CAP * nodes) + of_node[:1, :] * CAP + rank[:1, :]
        before = jnp.where(earlier < first_path, 1.0, 0.0).astype(BF16)
        row = jnp.dot(valid, before, preferred_element_type=F32)[:1, :]
        rows.append(jnp.where(filled, row, -1.0))
    return rows


def ring_way(chips):
    core, _ = other_core()
    me = (lax.axis_index("dp") - core) // 2
    return me, [{"dp": 2 * lax.rem(me + step + chips, chips) + core} for step in (1, -1)]


def ring_steps(
    chips, part, table, shares, values, got, stage, bounds, bounds_in, rsend, rrecv, gsend, grecv, vsend, vrecv, tsend, trecv
):
    me, way = ring_way(chips)
    depth = chips // 2
    half = SUBS // 2
    width = part.shape[3] // 3
    rows = part.shape[2]

    def chip(offset):
        return lax.rem(me + offset + 2 * chips, chips)

    sign = (1, -1)

    def halves(direction):
        return range(half) if direction == 0 else range(half, SUBS)

    copies = []

    def bound(ref, chunk):
        lines = [jnp.broadcast_to(ref[index, pl.ds(chunk, 1), :], (1, 128)) for index in range(3)]
        return jnp.concatenate([line for line in lines for _ in range(width // 128)], axis=1)

    def reduce_send(direction, step, sub, total, chunk):
        at = (direction, step, sub)
        limit = bound(bounds.at[direction, step], chunk)
        inverse = jnp.where(limit > 1e-30, STEPS / jnp.maximum(limit, 1e-30), 0.0)
        stage[at] = jnp.round(total * inverse).astype(jnp.int32).astype(jnp.int16)
        copies.append(push(stage.at[at], got.at[at], rsend.at[at], rrecv.at[at], way[direction]))

    def reduce_wait(direction, step, sub, chunk):
        at = (direction, step, sub)
        pltpu.make_async_copy(got.at[at], got.at[at], rrecv.at[at]).wait()
        limit = bound(bounds_in.at[direction, step], chunk)
        return got[at].astype(jnp.int32).astype(F32) * (limit * (1.0 / STEPS))

    def bound_send(direction, step):
        at = (direction, step)
        copies.append(push(bounds.at[at], bounds_in.at[at], tsend.at[at], trecv.at[at], way[direction]))

    def bound_wait(direction, step):
        at = (direction, step)
        pltpu.make_async_copy(bounds_in.at[at], bounds_in.at[at], trecv.at[at]).wait()

    for direction in range(2):
        bounds[direction, 0] = table[...]
        bound_send(direction, 0)
    for index in range(half):
        for direction in range(2):
            sub = halves(direction)[index]
            chunk = chip(sign[direction] * depth)
            reduce_send(direction, 0, sub, part[sub, chunk], chunk)
    for step in range(1, depth):
        for direction in range(2):
            bound_wait(direction, step - 1)
            bounds[direction, step] = table[...] + bounds_in[direction, step - 1]
            bound_send(direction, step)
        for index in range(half):
            for direction in range(2):
                if step == 1:
                    sub = halves(1 - direction)[index]
                    chunk = chip(sign[direction] * (depth - 1))
                    reduce_send(direction, 1, sub, part[sub, chunk], chunk)
        for sub in range(SUBS):
            for direction in range(2):
                if step == 1 and sub not in halves(direction):
                    continue
                chunk = chip(sign[direction] * (depth - step))
                total = part[sub, chunk] + reduce_wait(direction, step - 1, sub, chunk)
                reduce_send(direction, step, sub, total, chunk)
    for direction in range(2):
        bound_wait(direction, depth - 1)

    def gather_send(direction, step, sub):
        chunk = shares.at[sub, chip(-sign[direction] * step)]
        at = (direction, step, sub)
        copies.append(push(chunk, chunk, gsend.at[at], grecv.at[at], way[direction]))

    def gather_wait(direction, step, sub):
        chunk = shares.at[sub, chip(-sign[direction] * (step + 1))]
        pltpu.make_async_copy(chunk, chunk, grecv.at[direction, step, sub]).wait()

    def value_send(direction, step):
        chunk = values.at[chip(-sign[direction] * step)]
        at = (direction, step)
        copies.append(push(chunk, chunk, vsend.at[at], vrecv.at[at], way[direction]))

    def value_wait(direction, step):
        chunk = values.at[chip(-sign[direction] * (step + 1))]
        pltpu.make_async_copy(chunk, chunk, vrecv.at[direction, step]).wait()

    inner = jnp.zeros((rows, 1), F32)
    for index in range(half):
        for sub in (halves(0)[index], halves(1)[index]):
            total = part[sub, me]
            for direction in range(2):
                if depth > 1 or sub in halves(direction):
                    total = total + reduce_wait(direction, depth - 1, sub, me)
            gate, up, back = total[:, :width], total[:, width : 2 * width], total[:, 2 * width :]
            logistic = 1.0 / (1.0 + jnp.exp(-gate))
            active = gate * logistic
            hidden = (active * up).astype(BF16)
            shares[sub, me, :, :width] = hidden
            d_gate = back * up * logistic * (1.0 + gate * (1.0 - logistic))
            shares[sub, me, :, width : 2 * width] = d_gate.astype(BF16)
            shares[sub, me, :, 2 * width :] = (back * active).astype(BF16)
            for direction in range(2):
                if depth > 1 or sub in halves(direction):
                    gather_send(direction, 0, sub)
            inner = inner + jnp.sum(hidden.astype(F32) * back, axis=1, keepdims=True)
    lanes = lax.broadcasted_iota(jnp.int32, (rows, 128), 1)
    diagonal = lax.broadcasted_iota(jnp.int32, (rows, 128), 0) == lanes
    line = jnp.sum(jnp.where(diagonal, inner, 0.0), axis=0, keepdims=True)
    values[me] = jnp.broadcast_to(line, (8, 128))
    for direction in range(2):
        if depth > 1 or direction == 0:
            value_send(direction, 0)
    for step in range(1, depth + 1):
        last = step == depth
        for index in range(half):
            for sub in (halves(0)[index], halves(1)[index]):
                for direction in range(2):
                    if last and sub not in halves(direction):
                        continue
                    gather_wait(direction, step - 1, sub)
                    if not last and (step < depth - 1 or sub in halves(direction)):
                        gather_send(direction, step, sub)
        for direction in range(2):
            if last and direction == 1:
                continue
            value_wait(direction, step - 1)
            if not last and (step < depth - 1 or direction == 0):
                value_send(direction, step)
    return copies


def first_products(chips, place, toks, cots, weights, rows_of, part, table):
    rows, slots = rows_of.shape[2], toks.shape[1]
    wg, wu, wd, wg2, wu2, wd2 = weights
    width = wg.shape[1] // SUBS
    table[...] = jnp.zeros_like(table)
    row = lax.broadcasted_iota(jnp.int32, (rows, slots), 0).astype(F32)
    for path, src in enumerate((toks, cots)):
        pack = jnp.where(row == place[path], 1.0, 0.0).astype(BF16)
        for side in range(2):
            rows_of[path, side] = jnp.dot(pack, src[side], preferred_element_type=F32).astype(BF16)
    for sub in range(SUBS):
        units = slice(sub * width, (sub + 1) * width)
        gate = jnp.dot(rows_of[0, 0], wg[:, units], preferred_element_type=F32)
        gate = gate + jnp.dot(rows_of[0, 1], wg2[:, units], preferred_element_type=F32)
        up = jnp.dot(rows_of[0, 0], wu[:, units], preferred_element_type=F32)
        up = up + jnp.dot(rows_of[0, 1], wu2[:, units], preferred_element_type=F32)
        back = lax.dot_general(rows_of[1, 0], wd[units, :], NT, preferred_element_type=F32)
        back = back + lax.dot_general(rows_of[1, 1], wd2[units, :], NT, preferred_element_type=F32)
        for index, value in enumerate((gate, up, back)):
            value = value.reshape(chips, rows // chips, width)
            part[sub, :, :, index * width : (index + 1) * width] = value
            top = jnp.max(jnp.max(jnp.abs(value), axis=1), axis=1, keepdims=True)
            table[index] = jnp.maximum(table[index], top)


def gather_gates(top, nodes, rows, routes, name, hit, vback, count, gates_out):
    experts, slots = hit.shape[:2]
    lanes = lax.broadcasted_iota(jnp.int32, (experts, slots, 128), 2)
    diagonal = lax.broadcasted_iota(jnp.int32, (experts, slots, 128), 1) == lanes
    value = jnp.sum(jnp.where(diagonal, vback[:, 0:1, :], 0.0), axis=2, keepdims=True)
    inner = jnp.sum(jnp.where(hit, value, 0.0), axis=1)
    number = jnp.sum(count[:experts, :], axis=1, keepdims=True)
    inner = inner + BALANCE * 2 / (top * rows) * number
    gates = [jnp.sum(jnp.where(routes[k : k + 1, :] == name, inner, 0.0), axis=0, keepdims=True) for k in range(top)]
    gates = jnp.concatenate(gates, axis=0)
    gates_out[...] = jnp.zeros_like(gates_out)
    for i in range(nodes):
        gates_out[i, :, :rows] = gates[:, i * rows : (i + 1) * rows]


def combine(path, top, nodes, locals_, meta, src, out):
    experts, slots, wide = src.shape
    rows = out.shape[1]
    weights, routes = lay_out(meta, top, rows)
    columns = routes.shape[1]
    name, _, code = slot_codes(rows, top, routes, names_of(path, nodes, locals_))
    weight = jnp.zeros((experts, columns), F32)
    for k in range(top):
        weight = weight + jnp.where(routes[k : k + 1, :] == name, weights[k : k + 1, :], 0.0)
    place = lax.broadcasted_iota(jnp.int32, (1, slots, 1), 1).astype(F32)
    hit = code[:, None, :] == place
    rows_back = src[...].reshape(experts * slots, wide)
    high = weight.astype(BF16).astype(F32)
    total = jnp.zeros((columns, wide), F32)
    for share in (high, weight - high):
        spread_ = jnp.where(hit, share[:, None, :], 0.0).astype(BF16).reshape(experts * slots, columns)
        total = total + lax.dot_general(spread_, rows_back, (((0,), (0,)), ((), ())), preferred_element_type=F32)
    out[...] = total.astype(BF16).reshape(out.shape)
    return routes, name, hit


def main_kernel(
    chips, nodes, locals_, counts, count_sum, toks, cots, metaz, metal, wg_all, wu_all, wd_all, wg2, wu2, wd2,
    forward_home, back_home, gates_home,
    wg, wu, wd, rows_of, part, table, shares, values, got, stage, bounds, bounds_in,
    forward_out, back_out, values_out, forward_in, back_in, values_in, forward_sum, back_sum, gates_sum,
    wsem, rsend, rrecv, gsend, grecv, vsend, vrecv, tsend, trecv, bsend, brecv, lsend, lrecv, hsend, hrecv,
):
    core, ways, everyone = paths_of(nodes, locals_)
    top, rows = metaz.shape[1] // 2, forward_home.shape[1]
    load = []
    for index, (src, dst) in enumerate(((wg_all, wg), (wu_all, wu), (wd_all, wd))):
        load.append(pltpu.make_async_copy(src.at[core], dst, wsem.at[index]))
        load[-1].start()
    here, way = ring_way(chips)
    greet(everyone + way)
    mine = 2 * ways[0][0] + core
    own = counts[:, pl.ds(mine, 1), :].reshape(locals_, 128)
    place = places(nodes, locals_, own)
    for copy in load:
        copy.wait()
    first_products(chips, place, toks, cots, (wg, wu, wd, wg2, wu2, wd2), rows_of, part, table)
    ring_copies = ring_steps(
        chips, part, table, shares, values, got, stage, bounds, bounds_in,
        rsend, rrecv, gsend, grecv, vsend, vrecv, tsend, trecv,
    )
    count, slots = rows_of.shape[2], toks.shape[1]
    features, hidden = wg2.shape
    width = hidden // SUBS
    share = count // chips
    value = jnp.concatenate([upright(values[chip, 0:1, :], share) for chip in range(chips)], axis=0)
    row = lax.broadcasted_iota(jnp.int32, (count, slots), 0).astype(F32)
    value = jnp.sum(jnp.where(row == place[0], value, 0.0), axis=0, keepdims=True)
    values_out[...] = jnp.zeros_like(values_out)
    span = slots // locals_
    for relay in range(locals_):
        values_out[relay, :, :span] = jnp.broadcast_to(value[:, relay * span : (relay + 1) * span], (8, span))
    row = lax.broadcasted_iota(jnp.int32, (slots, count), 1).astype(F32)

    def kind(sub, index):
        return shares[sub, :, :, index * width : (index + 1) * width].reshape(count, width)

    copies = [[], []]
    for path, (out, dst) in enumerate(((forward_out, forward_in), (back_out, back_in))):
        unpack = jnp.where(row == upright(place[path], slots), 1.0, 0.0).astype(BF16)
        me, at, same, cross = ways[path]
        for side, (gate, up, down) in enumerate(((wg, wu, wd), (wg2, wu2, wd2))):
            total = jnp.zeros((count, features), F32)
            for sub in range(SUBS):
                units = slice(sub * width, (sub + 1) * width)
                if path == 0:
                    total = total + jnp.dot(kind(sub, 0), down[units, :], preferred_element_type=F32)
                else:
                    total = total + lax.dot_general(kind(sub, 1), gate[:, units], NT, preferred_element_type=F32)
                    total = total + lax.dot_general(kind(sub, 2), up[:, units], NT, preferred_element_type=F32)
            back = jnp.dot(unpack, total.astype(BF16), preferred_element_type=F32).astype(BF16)
            out[side] = back.reshape(out.shape[1:])
            peers = same if side == 0 else cross
            for step in list(range(1, len(at))) + [0]:
                if step == 0 and side == 0:
                    continue
                sem = (path, step, side)
                copies[path].append(
                    push(out.at[side, at[step]], dst.at[2 * me + core], bsend.at[sem], brecv.at[sem], peers[step])
                )
                if path == 0:
                    sem = (step, side)
                    line, slot = values_out.at[at[step]], values_in.at[2 * me + core]
                    copies[path].append(push(line, slot, lsend.at[sem], lrecv.at[sem], peers[step]))
        dst[2 * me + core] = out[0, me]
        if path == 0:
            values_in[2 * me + core] = values_out[me]

    homeward = []
    for path, (meta, src, out, dst) in enumerate(
        ((metaz, forward_in, forward_sum, forward_home), (metal, back_in, back_sum, back_home))
    ):
        for copy in copies[path]:
            copy.wait_recv()
        routes, name, hit = combine(path, top, nodes, locals_, meta, src, out)
        me, at, peers, _ = ways[1 - path]
        for step in range(1, len(at)):
            sem = (step, path)
            homeward.append(push(out.at[at[step]], dst.at[step], hsend.at[sem], hrecv.at[sem], peers[step]))
        dst[0] = out[me]
        if path == 0:
            gather_gates(top, nodes, rows, routes, name, hit, values_in, count_sum, gates_sum)
            for step in range(1, len(at)):
                sem = (step, 2)
                homeward.append(
                    push(gates_sum.at[at[step]], gates_home.at[step], hsend.at[sem], hrecv.at[sem], peers[step])
                )
            gates_home[0] = gates_sum[me]
    for copy in homeward:
        copy.wait()
    for copy in copies[0] + copies[1] + ring_copies:
        copy.wait_send()


def main(chips, nodes, locals_, count, ident, counts, count_sum, toks, cots, metaz, metal, rows, wg, wu, wd, wg2, wu2, wd2):
    top = metaz.shape[1] // 2
    _, slots, features = toks.shape
    wide = 3 * (wg.shape[2] // SUBS)
    depth = chips // 2
    share = count // chips
    most = max(nodes, locals_)
    table = (3, chips, 128)
    forward = (2, locals_, nodes * CAP, features)
    back = (2, nodes, locals_ * CAP, features)
    homes = [((nodes, rows, features), BF16), ((locals_, rows, features), BF16), ((nodes, top, 128), F32)]
    dma = pltpu.SemaphoreType.DMA
    return pl.pallas_call(
        functools.partial(main_kernel, chips, nodes, locals_),
        out_shape=[jax.ShapeDtypeStruct(*one) for one in homes],
        in_specs=[VMEM] * 6 + [ANY] * 3 + [VMEM] * 3,
        out_specs=[VMEM] * 3,
        scratch_shapes=[pltpu.VMEM(w.shape, BF16) for w in (wg2, wu2, wd2)]
        + [
            pltpu.VMEM((2, 2, count, features), BF16),
            pltpu.VMEM((SUBS, chips, share, wide), F32),
            pltpu.VMEM(table, F32),
            pltpu.VMEM((SUBS, chips, share, wide), BF16),
            pltpu.VMEM((chips, 8, 128), F32),
            pltpu.VMEM((2, depth, SUBS, share, wide), jnp.int16),
            pltpu.VMEM((2, depth, SUBS, share, wide), jnp.int16),
            pltpu.VMEM((2, depth) + table, F32),
            pltpu.VMEM((2, depth) + table, F32),
            pltpu.VMEM(forward, BF16),
            pltpu.VMEM(back, BF16),
            pltpu.VMEM((locals_, 8, 128), F32),
            pltpu.VMEM((2 * locals_,) + forward[2:], BF16),
            pltpu.VMEM((2 * nodes,) + back[2:], BF16),
            pltpu.VMEM((2 * locals_, 8, 128), F32),
        ]
        + [pltpu.VMEM(*one) for one in homes]
        + [dma((3,))]
        + [dma((2, depth, SUBS))] * 4
        + [dma((2, depth))] * 4
        + [dma((2, most, 2))] * 2
        + [dma((locals_, 2))] * 2
        + [dma((most, 3))] * 2,
        compiler_params=pltpu.CompilerParams(collective_id=ident, has_side_effects=True, vmem_limit_bytes=LIMIT),
    )(counts, count_sum, toks, cots, metaz, metal, wg, wu, wd, wg2, wu2, wd2)


def total_kernel(forward, back, gates, mixed, grads, gates_out):
    mixed[...] = jnp.sum(forward[...].astype(F32), axis=0).astype(BF16)
    grads[...] = jnp.sum(back[...].astype(F32), axis=0).astype(BF16)
    gates_out[...] = jnp.sum(gates[...], axis=0)[:, : gates_out.shape[1]]


def total(forward, back, gates):
    _, rows, features = forward.shape
    half = jax.ShapeDtypeStruct((rows, features), BF16)
    return pl.pallas_call(
        total_kernel,
        out_shape=[half, half, jax.ShapeDtypeStruct((gates.shape[1], rows), F32)],
        in_specs=[VMEM] * 3,
        out_specs=[VMEM] * 3,
        compiler_params=pltpu.CompilerParams(vmem_limit_bytes=LIMIT),
    )(forward, back, gates)


def body(chips, nodes, locals_, tokens, cotangent, routes, gate_weights, w_gate, w_up, w_down):
    rows, features = tokens.shape
    slots = nodes * locals_ * CAP
    toks, cots, counts, count_sum, metaz, metal, *swapped = front(
        nodes, locals_, tokens, cotangent, gate_weights.T, routes.T, w_gate, w_up, w_down
    )
    toks, cots = toks.reshape(2, slots, features), cots.reshape(2, slots, features)

    def sized(count, ident):
        def call(*operands):
            return main(chips, nodes, locals_, count, ident, *operands[:6], rows, *operands[6:])

        return call

    crowded = jnp.max(count_sum[2 * locals_ :, :]) > USUAL * chips
    operands = (counts, count_sum, toks, cots, metaz, metal, w_gate, w_up, w_down, *swapped)
    sums = lax.cond(crowded, sized(slots, 2), sized(USUAL * chips, 1), *operands)
    mixed, grads, gates = total(*sums)
    return mixed, grads, gates.T


def solution(mesh):
    chips, nodes, locals_ = mesh.shape["dp"] // 2, mesh.shape["node"], mesh.shape["local"]
    placed = (
        P(("node", "local"), "dp"),
        P(("node", "local"), "dp"),
        P(("node", "local"), None),
        P(("node", "local"), None),
        P(("node", "local"), "dp", None),
        P(("node", "local"), "dp", None),
        P(("node", "local"), None, "dp"),
    )
    return jax.shard_map(
        functools.partial(body, chips, nodes, locals_),
        mesh=mesh,
        in_specs=placed,
        out_specs=(
            P(("node", "local"), "dp"),
            P(("node", "local"), "dp"),
            P(("node", "local"), None),
        ),
        check_vma=False,
    )
```

time: 317 us -> 120 us (0.38)
  waiting for transfers between devices: 134 us -> 0 us
  Pallas kernels: 0 us -> 118 us
  blocking collectives: 114 us -> 0 us
  starting transfers between devices: 18.9 us -> 0 us
  local copies, waits for them, and re-layouts: 13.4 us -> 0.01 us
  between operations: 14.3 us -> 1.35 us
  other arithmetic: 12.1 us -> 0.6 us
  matrix products: 8.21 us -> 0 us
    pallas_call x0 -> x3, Pallas kernels: none -> 118 us  [the longest x1 69.6 us: main(): pl.pallas_call(functools.partial(main_kernel, chips, nodes, locals_), out...]
    reduce_scatter x1 -> x0, waiting for transfers between devices: 73.8 us -> none  [body(): lax.psum_scatter(jnp.stack([gate_part, up_part, back_part], axis=2), 'dp'...]
    all_to_all x2 -> x0, blocking collectives: 68.6 us -> none  [the longest x1 45.6 us: body(): lax.all_to_all(outgoing, ('node', 'local'), split_axis=0, concat_axis=0,...]
    psum x1 -> x0, blocking collectives: 45.2 us -> none  [body(): inner_dot = lax.psum(partial_dot, 'dp')]
    all_to_all x2 -> x0, waiting for transfers between devices: 38.4 us -> none  [the longest x1 38.4 us: body(): lax.all_to_all(results, ('node', 'local'), split_axis=0, concat_axis=0, t...]
    all_gather x1 -> x0, waiting for transfers between devices: 21.8 us -> none  [body(): piece_rows = lax.all_gather(shares, 'dp', axis=0, tiled=True)]
    all_to_all x2 -> x0, starting transfers between devices: 18.8 us -> none  [the longest x1 14.3 us: body(): lax.all_to_all(results, ('node', 'local'), split_axis=0, concat_axis=0, t...]
    dot_general x6 -> x0, matrix products: 8.21 us -> none  [the longest x1 2.18 us: body(): jnp.einsum('seh,ehj->sej', piece_rows[:, :, 0], w_down, preferred_element...]
  transfers between devices with their start and end apart: 4 -> 0, of which waited for: 3 -> 0; matrix products, arithmetic and copies ran while one was open for 3% -> 0% of each run, Pallas kernels for 0% -> 0%
where the time goes in v3:
time: 120 us
  Pallas kernels  118 us (98%)
  between operations  1.35 us (1%)
    pallas_call x1, Pallas kernels, main(): pl.pallas_call(functools.partial(main_kernel, chips, nodes, locals_), out...  69.6 us
    pallas_call x1, Pallas kernels, front(): pl.pallas_call(functools.partial(front_kernel, nodes, locals_), out_shape...  46.3 us

profile of v3, /device:TPU:1, one launch (start us, length us, event | category | flops | bytes accessed | tf_op | source)
XLA Modules:
  0.0 119.7 jit_solution(6317310836883732930)
XLA Ops:
  0.6 0.0 copy-start
  0.6 0.0 copy-start.1
  0.7 0.0 copy-start.2
  0.7 46.3 %shard_map.94 = (bf16[2,8,48,256]{3,2,1,0:T(8,128)(2,1)S(1)}, bf16[2,8,48,256]{3,2,1,0:T(8,128)(2,1)}, f32[8,24,128]{2,1,0:T(8,128)}, f32[24,128]{1,0:T(8,128)S(...) custom-call(bf16[48,256]{1,0:T(8,128)(2,1)} %tok.1, ...), custom_call_target="tpu_custom_call" | custom-call | tf_op jit(solution)/shard_map/pallas_call | solution.py:188
  46.9 0.6 slice_reduce_fusion
  48.2 0.0 copy-done
  48.2 0.0 copy-done.1
  48.2 0.0 copy-done.2
  48.2 69.8 %conditional.1 = ((bf16[8,48,256]{2,1,0:T(8,128)(2,1)}, bf16[8,48,256]{2,1,0:T(8,128)(2,1)}, f32[8,8,128]{2,1,0:T(8,128)})) conditional(s32[]{:T(128)} %convert_element_type.3, (f32[8,24,128]{2,1,0:T(8,128)}, f32[24,128]{1,0:T(8,128)S(1)}, bf16[2,384,256]{2,1,0:T(8,128)(2,1)S(1)}, bf16[2,384,256]{2,1,0:T(8,128)(2,1)}, f32[8,16,128]{2,1,0:T(8,128)}, ...), branch_computations={%region_1.0_spmd, %region_2.0_spmd} | conditional | bytes 8 | solution.py:627
  48.2 69.6 %branch_0_fun.1 = (bf16[8,48,256]{2,1,0:T(8,128)(2,1)}, bf16[8,48,256]{2,1,0:T(8,128)(2,1)}, f32[8,8,128]{2,1,0:T(8,128)}) custom-call(f32[8,24,128]{2,1,0:T(8,128)} %get-tuple-element.48.counts, f32[24,128]{1,0:T(8,128)S(1)} %get-tuple-element.49.count_sum, bf16[2,384,256]{2,1,0:T(8,128)(2,1)S(1)} %get-tuple-element.50.toks, ...), custom_call_target="tpu_custom_call" | custom-call | tf_op jit(solution)/shard_map/cond/branch_0_fun/pallas_call | solution.py:559
  118.0 1.7 %shard_map.95 = (bf16[48,256]{1,0:T(8,128)(2,1)}, bf16[48,256]{1,0:T(8,128)(2,1)}, f32[8,48]{1,0:T(8,128)}) custom-call(bf16[8,48,256]{2,1,0:T(8,128)(2,1)} %get-tuple-element.99.forward, bf16[8,48,256]{2,1,0:T(8,128)(2,1)} %get-tuple-element.100.back, f32[8,8,128]{2,1,0:T(8,128)} %get-tuple-element.101.gates), custom_call_target="tpu_custom_call" | custom-call | tf_op jit(solution)/shard_map/pallas_call | solution.py:602
Async XLA Ops:
  0.6 47.5 %copy-start = (bf16[2,256,1024]{2,1,0:T(8,128)(2,1)S(1)}, bf16[2,256,1024]{2,1,0:T(8,128)(2,1)}, u32[]{:S(2)}) copy-start(bf16[2,256,1024]{2,1,0:T(8,128)(2,1)} %wg.1) | copy-start | bytes 3145732
  0.6 47.5 %copy-start.1 = (bf16[2,256,1024]{2,1,0:T(8,128)(2,1)S(1)}, bf16[2,256,1024]{2,1,0:T(8,128)(2,1)}, u32[]{:S(2)}) copy-start(bf16[2,256,1024]{2,1,0:T(8,128)(2,1)} %wu.1) | copy-start | bytes 3145732
  0.7 47.5 %copy-start.2 = (bf16[2,1024,256]{2,1,0:T(8,128)(2,1)S(1)}, bf16[2,1024,256]{2,1,0:T(8,128)(2,1)}, u32[]{:S(2)}) copy-start(bf16[2,1024,256]{2,1,0:T(8,128)(2,1)} %wd.1) | copy-start | bytes 3145732

commit v4 on v3

--- a/solution.py
+++ b/solution.py
@@ -19,11 +19,14 @@
 LIMIT = 56 * 1024 * 1024
 
 
-def greet(peers):
+def hail(peers):
     barrier = pltpu.get_barrier_semaphore()
     for peer in peers:
         pl.semaphore_signal(barrier, inc=1, device_id=peer, device_id_type=MESH)
-    pl.semaphore_wait(barrier, len(peers))
+
+
+def await_all(peers):
+    pl.semaphore_wait(pltpu.get_barrier_semaphore(), len(peers))
 
 
 def push(src, dst, send, recv, peer):
@@ -86,7 +89,7 @@
 def lay_out(meta, top, rows):
     blocks = meta.shape[0]
     weights = jnp.concatenate([meta[i, :top, :rows] for i in range(blocks)], axis=1)
-    routes = jnp.concatenate([meta[i, top : 2 * top, :rows] for i in range(blocks)], axis=1)
+    routes = jnp.concatenate([meta[i, :top, 64 : 64 + rows] for i in range(blocks)], axis=1)
     return weights, routes
 
 
@@ -100,16 +103,12 @@
     return core, ways, peers
 
 
-def choose(path, top, nodes, locals_, src, meta, dst, count):
-    rows, features = src.shape[1:]
-    experts, slots, _ = dst.shape
+def pick_rows(path, top, nodes, locals_, rows, meta, experts, slots, count):
     _, routes = lay_out(meta, top, rows)
     columns = routes.shape[1]
     _, chosen, code = slot_codes(rows, top, routes, names_of(path, nodes, locals_))
     place = lax.broadcasted_iota(jnp.int32, (1, slots, 1), 1).astype(F32)
     pick = jnp.where(code[:, None, :] == place, 1.0, 0.0).astype(BF16).reshape(experts * slots, columns)
-    got = jnp.dot(pick, src[...].reshape(columns, features), preferred_element_type=F32)
-    dst[...] = got.astype(BF16).reshape(experts, slots, features)
     if path == 0:
         block = (lax.broadcasted_iota(jnp.int32, (columns, 128), 0) * -(-32768 // rows)) >> 15
         by_block = jnp.where(block == lax.broadcasted_iota(jnp.int32, (columns, 128), 1), 1.0, 0.0).astype(BF16)
@@ -120,24 +119,16 @@
         for k in range(top):
             hits = hits + jnp.where(routes[k : k + 1, :] == name, 1.0, 0.0)
         count[experts:, :] = jnp.broadcast_to(lying(jnp.sum(hits, axis=1, keepdims=True), 128), (8, 128))
-
-
-def front_kernel(
-    nodes, locals_, tok, cot, gates, routes, wg, wu, wd,
-    tok_in, cot_in, counts, count_sum, metaz, metal, wg2, wu2, wd2,
-    meta, tokz, cotl, tok_out, cot_out, count, send, recv, wsend, wrecv, ssend, srecv, csend, crecv,
+    return pick
+
+
+def front_steps(
+    nodes, locals_, ways, core, tok, cot, gates, routes, tok_in, cot_in, counts, count_sum, metaz, metal, swap,
+    meta, tokz, cotl, tok_out, cot_out, count, send, recv, ssend, srecv, csend, crecv,
 ):
-    node, nodes_at = ring_of("node", nodes)
-    place, locals_at = ring_of("local", locals_)
-    core, twin = other_core()
+    place, _, side, _ = ways[0]
+    node, _, far, _ = ways[1]
     top, rows = gates.shape
-    meta[...] = jnp.zeros_like(meta)
-    meta[:top, :rows] = gates[...]
-    meta[top:, :rows] = routes[...].astype(F32)
-    far = [{"node": at} for at in nodes_at]
-    side = [{"local": at} for at in locals_at]
-    core, ways, everyone = paths_of(nodes, locals_)
-    greet(everyone)
     blocks = [[], []]
     for step in range(1, max(nodes, locals_)):
         for path, (peers, me, arrays) in enumerate(
@@ -146,71 +137,114 @@
             if step < len(peers):
                 for index, (src, dst) in enumerate(arrays):
                     at = (path, step - 1, index)
-                    blocks[path].append(push(src, dst.at[me], send.at[at], recv.at[at], peers[step]))
+                    blocks[index].append((path, push(src, dst.at[me], send.at[at], recv.at[at], peers[step])))
+    swap()
     tokz[node] = tok[...]
     cotl[place] = cot[...]
     metaz[node] = meta[...]
     metal[place] = meta[...]
-    copies = []
-    for path, (src, met, out, dst) in enumerate(((tokz, metaz, tok_out, tok_in), (cotl, metal, cot_out, cot_in))):
-        for copy in blocks[path]:
-            copy.wait_recv()
-        choose(path, top, nodes, locals_, src, met, out, count)
-        me, at, same, cross = ways[path]
+    picks, numbers, copies = [], [], [[], []]
+    for path, (met, out) in enumerate(((metaz, tok_out), (metal, cot_out))):
+        for which, copy in blocks[0]:
+            if which == path:
+                copy.wait_recv()
+        picks.append(pick_rows(path, top, nodes, locals_, rows, met, out.shape[0], out.shape[1], count))
         if path == 0:
             for step in range(1, locals_):
                 sem = step - 1
-                copies.append(push(count, counts.at[me], csend.at[sem], crecv.at[sem], same[step]))
+                numbers.append(push(count, counts.at[place], csend.at[sem], crecv.at[sem], side[step]))
+            counts[place] = count[...]
+    for path, (src, out, dst) in enumerate(((tokz, tok_out, tok_in), (cotl, cot_out, cot_in))):
+        for which, copy in blocks[1]:
+            if which == path:
+                copy.wait_recv()
+        picked = jnp.dot(picks[path], src[...].reshape(-1, src.shape[2]), preferred_element_type=F32)
+        out[...] = picked.astype(BF16).reshape(out.shape)
+        me, at, same, cross = ways[path]
         for step in list(range(1, len(at))) + [0]:
             for distant, peers in enumerate((same, cross)):
                 if step == 0 and distant == 0:
                     continue
                 expert = 2 * at[step] + (core if distant == 0 else 1 - core)
                 sem = (path, step, distant)
-                copies.append(push(out.at[expert], dst.at[distant, me], ssend.at[sem], srecv.at[sem], peers[step]))
+                copies[path].append(push(out.at[expert], dst.at[distant, me], ssend.at[sem], srecv.at[sem], peers[step]))
         dst[0, me] = out[2 * me + core]
-    counts[place] = count[...]
-    for index, (src, dst) in enumerate(((wg, wg2), (wu, wu2), (wd, wd2))):
-        copies.append(push(src.at[1 - core], dst, wsend.at[index], wrecv.at[index], {"dp": twin}))
-    for copy in copies:
+    return numbers, copies[0], copies[1], [copy for _, copy in blocks[0] + blocks[1]]
+
+
+def fill_meta(gates, routes, meta):
+    top, rows = gates.shape
+    meta[...] = jnp.zeros_like(meta)
+    meta[:, :rows] = gates[...]
+    meta[:, 64 : 64 + rows] = routes[...].astype(F32)
+
+
+def front_kernel(
+    nodes, locals_, tok, cot, gates, routes, wg, wu, wd,
+    tok_in, cot_in, counts, count_sum, metaz, metal, wg2, wu2, wd2, wsend, wrecv, meta, *scratch,
+):
+    core, ways, everyone = paths_of(nodes, locals_)
+    _, twin = other_core()
+    fill_meta(gates, routes, meta)
+    hail(everyone)
+    await_all(everyone)
+    copies = []
+
+    def swap():
+        for index, (src, dst) in enumerate(((wg, wg2), (wu, wu2), (wd, wd2))):
+            copies.append(push(src.at[1 - core], dst, wsend.at[index], wrecv.at[index], {"dp": twin}))
+
+    numbers, toks, cots, blocks = front_steps(
+        nodes, locals_, ways, core, tok, cot, gates, routes, tok_in, cot_in, counts, count_sum, metaz, metal, swap,
+        meta, *scratch,
+    )
+    for copy in copies + numbers + toks + cots:
         copy.wait()
-    for path in range(2):
-        for copy in blocks[path]:
-            copy.wait_send()
+    for copy in blocks:
+        copy.wait_send()
     count_sum[...] = jnp.sum(counts[...], axis=0)
 
 
+def front_shapes(nodes, locals_, features, top):
+    meta, count = (top, 128), (2 * locals_ + 8, 128)
+    return [
+        ((2, locals_, nodes * CAP, features), BF16),
+        ((2, nodes, locals_ * CAP, features), BF16),
+        ((locals_,) + count, F32),
+        (count, F32),
+        ((nodes,) + meta, F32),
+        ((locals_,) + meta, F32),
+    ]
+
+
+def front_scratch(nodes, locals_, rows, features, top):
+    most = max(nodes, locals_)
+    dma = pltpu.SemaphoreType.DMA
+    return (
+        [
+            pltpu.VMEM((top, 128), F32),
+            pltpu.VMEM((nodes, rows, features), BF16),
+            pltpu.VMEM((locals_, rows, features), BF16),
+            pltpu.VMEM((2 * locals_, nodes * CAP, features), BF16),
+            pltpu.VMEM((2 * nodes, locals_ * CAP, features), BF16),
+            pltpu.VMEM((2 * locals_ + 8, 128), F32),
+        ]
+        + [dma((2, most, 2))] * 4
+        + [dma((locals_,))] * 2
+    )
+
+
 def front(nodes, locals_, tok, cot, gates, routes, wg, wu, wd):
-    features = tok.shape[1]
-    most = max(nodes, locals_)
-    meta = (2 * gates.shape[0], 128)
-    count = (2 * locals_ + 8, 128)
+    rows, features = tok.shape
+    top = gates.shape[0]
     return pl.pallas_call(
         functools.partial(front_kernel, nodes, locals_),
-        out_shape=[
-            jax.ShapeDtypeStruct((2, locals_, nodes * CAP, features), BF16),
-            jax.ShapeDtypeStruct((2, nodes, locals_ * CAP, features), BF16),
-            jax.ShapeDtypeStruct((locals_,) + count, F32),
-            jax.ShapeDtypeStruct(count, F32),
-            jax.ShapeDtypeStruct((nodes,) + meta, F32),
-            jax.ShapeDtypeStruct((locals_,) + meta, F32),
-        ]
+        out_shape=[jax.ShapeDtypeStruct(*one) for one in front_shapes(nodes, locals_, features, top)]
         + [jax.ShapeDtypeStruct(a.shape[1:], a.dtype) for a in (wg, wu, wd)],
         in_specs=[VMEM] * 4 + [ANY] * 3,
         out_specs=[VMEM] * 6 + [ANY] * 3,
-        scratch_shapes=[
-            pltpu.VMEM(meta, F32),
-            pltpu.VMEM((nodes,) + tok.shape, BF16),
-            pltpu.VMEM((locals_,) + cot.shape, BF16),
-            pltpu.VMEM((2 * locals_, nodes * CAP, features), BF16),
-            pltpu.VMEM((2 * nodes, locals_ * CAP, features), BF16),
-            pltpu.VMEM(count, F32),
-        ]
-        + [pltpu.SemaphoreType.DMA((2, most, 2))] * 2
-        + [pltpu.SemaphoreType.DMA((3,))] * 2
-        + [pltpu.SemaphoreType.DMA((2, most, 2))] * 2
-        + [pltpu.SemaphoreType.DMA((locals_,))] * 2,
-        compiler_params=pltpu.CompilerParams(collective_id=0, has_side_effects=True, vmem_limit_bytes=LIMIT),
+        scratch_shapes=[pltpu.SemaphoreType.DMA((3,))] * 2 + front_scratch(nodes, locals_, rows, features, top),
+        compiler_params=pltpu.CompilerParams(collective_id=1, has_side_effects=True, vmem_limit_bytes=LIMIT),
     )(tok, cot, gates, routes, wg, wu, wd)
 
 
@@ -250,7 +284,8 @@
 
 
 def ring_steps(
-    chips, part, table, shares, values, got, stage, bounds, bounds_in, rsend, rrecv, gsend, grecv, vsend, vrecv, tsend, trecv
+    chips, early, late, ready, part, table, shares, values, got, stage, bounds, bounds_in,
+    rsend, rrecv, gsend, grecv, vsend, vrecv, tsend, trecv,
 ):
     me, way = ring_way(chips)
     depth = chips // 2
@@ -269,8 +304,9 @@
     copies = []
 
     def bound(ref, chunk):
-        lines = [jnp.broadcast_to(ref[index, pl.ds(chunk, 1), :], (1, 128)) for index in range(3)]
-        return jnp.concatenate([line for line in lines for _ in range(width // 128)], axis=1)
+        line = ref[pl.ds(chunk, 1), :]
+        kinds = [jnp.broadcast_to(line[:, 32 * index : 32 * index + 1], (1, width)) for index in range(3)]
+        return jnp.concatenate(kinds, axis=1)
 
     def reduce_send(direction, step, sub, total, chunk):
         at = (direction, step, sub)
@@ -301,6 +337,7 @@
             sub = halves(direction)[index]
             chunk = chip(sign[direction] * depth)
             reduce_send(direction, 0, sub, part[sub, chunk], chunk)
+    early()
     for step in range(1, depth):
         for direction in range(2):
             bound_wait(direction, step - 1)
@@ -362,12 +399,20 @@
     lanes = lax.broadcasted_iota(jnp.int32, (rows, 128), 1)
     diagonal = lax.broadcasted_iota(jnp.int32, (rows, 128), 0) == lanes
     line = jnp.sum(jnp.where(diagonal, inner, 0.0), axis=0, keepdims=True)
-    values[me] = jnp.broadcast_to(line, (8, 128))
+    values[me] = line
     for direction in range(2):
         if depth > 1 or direction == 0:
             value_send(direction, 0)
     for step in range(1, depth + 1):
         last = step == depth
+        for direction in range(2):
+            if last and direction == 1:
+                continue
+            value_wait(direction, step - 1)
+            if not last and (step < depth - 1 or direction == 0):
+                value_send(direction, step)
+        if last:
+            late()
         for index in range(half):
             for sub in (halves(0)[index], halves(1)[index]):
                 for direction in range(2):
@@ -376,38 +421,37 @@
                     gather_wait(direction, step - 1, sub)
                     if not last and (step < depth - 1 or sub in halves(direction)):
                         gather_send(direction, step, sub)
-        for direction in range(2):
-            if last and direction == 1:
-                continue
-            value_wait(direction, step - 1)
-            if not last and (step < depth - 1 or direction == 0):
-                value_send(direction, step)
+                if last:
+                    ready(sub)
     return copies
 
 
-def first_products(chips, place, toks, cots, weights, rows_of, part, table):
-    rows, slots = rows_of.shape[2], toks.shape[1]
-    wg, wu, wd, wg2, wu2, wd2 = weights
-    width = wg.shape[1] // SUBS
-    table[...] = jnp.zeros_like(table)
-    row = lax.broadcasted_iota(jnp.int32, (rows, slots), 0).astype(F32)
-    for path, src in enumerate((toks, cots)):
-        pack = jnp.where(row == place[path], 1.0, 0.0).astype(BF16)
-        for side in range(2):
-            rows_of[path, side] = jnp.dot(pack, src[side], preferred_element_type=F32).astype(BF16)
+def pack_rows(place, src, dst):
+    _, rows, features = dst.shape
+    row = lax.broadcasted_iota(jnp.int32, (rows, place.shape[1]), 0).astype(F32)
+    pack = jnp.where(row == place, 1.0, 0.0).astype(BF16)
+    for side in range(2):
+        slots = src[side].reshape(-1, features)
+        dst[side] = jnp.dot(pack, slots, preferred_element_type=F32).astype(BF16)
+
+
+def first_products(chips, kinds, rows_of, part, table):
+    rows = rows_of.shape[1]
+    width = part.shape[3] // 3
+    lane_kind = lax.broadcasted_iota(jnp.int32, (chips, 128), 1) >> 5
     for sub in range(SUBS):
         units = slice(sub * width, (sub + 1) * width)
-        gate = jnp.dot(rows_of[0, 0], wg[:, units], preferred_element_type=F32)
-        gate = gate + jnp.dot(rows_of[0, 1], wg2[:, units], preferred_element_type=F32)
-        up = jnp.dot(rows_of[0, 0], wu[:, units], preferred_element_type=F32)
-        up = up + jnp.dot(rows_of[0, 1], wu2[:, units], preferred_element_type=F32)
-        back = lax.dot_general(rows_of[1, 0], wd[units, :], NT, preferred_element_type=F32)
-        back = back + lax.dot_general(rows_of[1, 1], wd2[units, :], NT, preferred_element_type=F32)
-        for index, value in enumerate((gate, up, back)):
+        for index, (own, twin) in kinds:
+            if index < 2:
+                value = jnp.dot(rows_of[0], own[:, units], preferred_element_type=F32)
+                value = value + jnp.dot(rows_of[1], twin[:, units], preferred_element_type=F32)
+            else:
+                value = lax.dot_general(rows_of[0], own[units, :], NT, preferred_element_type=F32)
+                value = value + lax.dot_general(rows_of[1], twin[units, :], NT, preferred_element_type=F32)
             value = value.reshape(chips, rows // chips, width)
             part[sub, :, :, index * width : (index + 1) * width] = value
             top = jnp.max(jnp.max(jnp.abs(value), axis=1), axis=1, keepdims=True)
-            table[index] = jnp.maximum(table[index], top)
+            table[...] = jnp.maximum(table[...], jnp.where(lane_kind == index, top, 0.0))
 
 
 def gather_gates(top, nodes, rows, routes, name, hit, vback, count, gates_out):
@@ -425,9 +469,7 @@
         gates_out[i, :, :rows] = gates[:, i * rows : (i + 1) * rows]
 
 
-def combine(path, top, nodes, locals_, meta, src, out):
-    experts, slots, wide = src.shape
-    rows = out.shape[1]
+def weigh(path, top, nodes, locals_, rows, meta, experts, slots):
     weights, routes = lay_out(meta, top, rows)
     columns = routes.shape[1]
     name, _, code = slot_codes(rows, top, routes, names_of(path, nodes, locals_))
@@ -436,71 +478,86 @@
         weight = weight + jnp.where(routes[k : k + 1, :] == name, weights[k : k + 1, :], 0.0)
     place = lax.broadcasted_iota(jnp.int32, (1, slots, 1), 1).astype(F32)
     hit = code[:, None, :] == place
-    rows_back = src[...].reshape(experts * slots, wide)
     high = weight.astype(BF16).astype(F32)
-    total = jnp.zeros((columns, wide), F32)
-    for share in (high, weight - high):
-        spread_ = jnp.where(hit, share[:, None, :], 0.0).astype(BF16).reshape(experts * slots, columns)
-        total = total + lax.dot_general(spread_, rows_back, (((0,), (0,)), ((), ())), preferred_element_type=F32)
-    out[...] = total.astype(BF16).reshape(out.shape)
-    return routes, name, hit
-
-
-def main_kernel(
-    chips, nodes, locals_, counts, count_sum, toks, cots, metaz, metal, wg_all, wu_all, wd_all, wg2, wu2, wd2,
-    forward_home, back_home, gates_home,
-    wg, wu, wd, rows_of, part, table, shares, values, got, stage, bounds, bounds_in,
+    shares = [
+        jnp.where(hit, share[:, None, :], 0.0).astype(BF16).reshape(experts * slots, columns).T
+        for share in (high, weight - high)
+    ]
+    return routes, name, hit, shares
+
+
+def main_steps(
+    chips, nodes, locals_, ways, core, ready_counts, ready_weights, ready_toks, ready_cots, ready_peers,
+    counts, count_sum, toks, cots, metaz, metal, forward_home, back_home, gates_home,
+    wg, wu, wd, wg2, wu2, wd2, unpack, sums, rows_of, part, table, shares, values, got, stage, bounds, bounds_in,
     forward_out, back_out, values_out, forward_in, back_in, values_in, forward_sum, back_sum, gates_sum,
-    wsem, rsend, rrecv, gsend, grecv, vsend, vrecv, tsend, trecv, bsend, brecv, lsend, lrecv, hsend, hrecv,
+    rsend, rrecv, gsend, grecv, vsend, vrecv, tsend, trecv, bsend, brecv, lsend, lrecv, hsend, hrecv,
 ):
-    core, ways, everyone = paths_of(nodes, locals_)
-    top, rows = metaz.shape[1] // 2, forward_home.shape[1]
-    load = []
-    for index, (src, dst) in enumerate(((wg_all, wg), (wu_all, wu), (wd_all, wd))):
-        load.append(pltpu.make_async_copy(src.at[core], dst, wsem.at[index]))
-        load[-1].start()
-    here, way = ring_way(chips)
-    greet(everyone + way)
+    top, rows = metaz.shape[1], forward_home.shape[1]
+    count = rows_of.shape[2]
+    slots = nodes * locals_ * CAP
+    features, hidden = wg2.shape
+    width = hidden // SUBS
+    share = count // chips
+    span = slots // locals_
+    table[...] = jnp.zeros_like(table)
+    ready_counts()
     mine = 2 * ways[0][0] + core
     own = counts[:, pl.ds(mine, 1), :].reshape(locals_, 128)
     place = places(nodes, locals_, own)
-    for copy in load:
-        copy.wait()
-    first_products(chips, place, toks, cots, (wg, wu, wd, wg2, wu2, wd2), rows_of, part, table)
-    ring_copies = ring_steps(
-        chips, part, table, shares, values, got, stage, bounds, bounds_in,
-        rsend, rrecv, gsend, grecv, vsend, vrecv, tsend, trecv,
-    )
-    count, slots = rows_of.shape[2], toks.shape[1]
-    features, hidden = wg2.shape
-    width = hidden // SUBS
-    share = count // chips
-    value = jnp.concatenate([upright(values[chip, 0:1, :], share) for chip in range(chips)], axis=0)
-    row = lax.broadcasted_iota(jnp.int32, (count, slots), 0).astype(F32)
-    value = jnp.sum(jnp.where(row == place[0], value, 0.0), axis=0, keepdims=True)
-    values_out[...] = jnp.zeros_like(values_out)
-    span = slots // locals_
-    for relay in range(locals_):
-        values_out[relay, :, :span] = jnp.broadcast_to(value[:, relay * span : (relay + 1) * span], (8, span))
-    row = lax.broadcasted_iota(jnp.int32, (slots, count), 1).astype(F32)
+    ready_weights()
+    ready_toks()
+    pack_rows(place[0], toks, rows_of.at[0])
+    first_products(chips, ((0, (wg, wg2)), (1, (wu, wu2))), rows_of.at[0], part, table)
+    ready_cots()
+    pack_rows(place[1], cots, rows_of.at[1])
+    first_products(chips, ((2, (wd, wd2)),), rows_of.at[1], part, table)
+    ready_peers()
+    value_copies = []
+
+    def early():
+        row = lax.broadcasted_iota(jnp.int32, (slots, count), 1).astype(F32)
+        for path in range(2):
+            unpack[path] = jnp.where(row == upright(place[path], slots), 1.0, 0.0).astype(BF16)
+
+    def late():
+        value = jnp.concatenate([upright(values[chip, 0:1, :], share) for chip in range(chips)], axis=0)
+        row = lax.broadcasted_iota(jnp.int32, (count, slots), 0).astype(F32)
+        value = jnp.sum(jnp.where(row == place[0], value, 0.0), axis=0, keepdims=True)
+        values_out[...] = jnp.zeros_like(values_out)
+        for relay in range(locals_):
+            values_out[relay, :, :span] = value[:, relay * span : (relay + 1) * span]
+        me, at, same, cross = ways[0]
+        for step in range(locals_):
+            for side, peers in enumerate((same, cross)):
+                if step == 0 and side == 0:
+                    continue
+                sem = (step, side)
+                line, slot = values_out.at[at[step]], values_in.at[2 * me + core]
+                value_copies.append(push(line, slot, lsend.at[sem], lrecv.at[sem], peers[step]))
+        values_in[2 * me + core] = values_out[me]
+        sums[...] = jnp.zeros_like(sums)
 
     def kind(sub, index):
         return shares[sub, :, :, index * width : (index + 1) * width].reshape(count, width)
 
+    def ready(sub):
+        units = slice(sub * width, (sub + 1) * width)
+        for side, (gate, up, down) in enumerate(((wg, wu, wd), (wg2, wu2, wd2))):
+            sums[0, side] += jnp.dot(kind(sub, 0), down[units, :], preferred_element_type=F32)
+            back = lax.dot_general(kind(sub, 1), gate[:, units], NT, preferred_element_type=F32)
+            back = back + lax.dot_general(kind(sub, 2), up[:, units], NT, preferred_element_type=F32)
+            sums[1, side] += back
+
+    ring_copies = ring_steps(
+        chips, early, late, ready, part, table, shares, values, got, stage, bounds, bounds_in,
+        rsend, rrecv, gsend, grecv, vsend, vrecv, tsend, trecv,
+    )
     copies = [[], []]
     for path, (out, dst) in enumerate(((forward_out, forward_in), (back_out, back_in))):
-        unpack = jnp.where(row == upright(place[path], slots), 1.0, 0.0).astype(BF16)
         me, at, same, cross = ways[path]
-        for side, (gate, up, down) in enumerate(((wg, wu, wd), (wg2, wu2, wd2))):
-            total = jnp.zeros((count, features), F32)
-            for sub in range(SUBS):
-                units = slice(sub * width, (sub + 1) * width)
-                if path == 0:
-                    total = total + jnp.dot(kind(sub, 0), down[units, :], preferred_element_type=F32)
-                else:
-                    total = total + lax.dot_general(kind(sub, 1), gate[:, units], NT, preferred_element_type=F32)
-                    total = total + lax.dot_general(kind(sub, 2), up[:, units], NT, preferred_element_type=F32)
-            back = jnp.dot(unpack, total.astype(BF16), preferred_element_type=F32).astype(BF16)
+        for side in range(2):
+            back = jnp.dot(unpack[path], sums[path, side].astype(BF16), preferred_element_type=F32).astype(BF16)
             out[side] = back.reshape(out.shape[1:])
             peers = same if side == 0 else cross
             for step in list(range(1, len(at))) + [0]:
@@ -510,21 +567,24 @@
                 copies[path].append(
                     push(out.at[side, at[step]], dst.at[2 * me + core], bsend.at[sem], brecv.at[sem], peers[step])
                 )
-                if path == 0:
-                    sem = (step, side)
-                    line, slot = values_out.at[at[step]], values_in.at[2 * me + core]
-                    copies[path].append(push(line, slot, lsend.at[sem], lrecv.at[sem], peers[step]))
         dst[2 * me + core] = out[0, me]
-        if path == 0:
-            values_in[2 * me + core] = values_out[me]
-
+
+    weighed = [
+        weigh(path, top, nodes, locals_, rows, meta, src.shape[0], src.shape[1])
+        for path, (meta, src) in enumerate(((metaz, forward_in), (metal, back_in)))
+    ]
     homeward = []
-    for path, (meta, src, out, dst) in enumerate(
-        ((metaz, forward_in, forward_sum, forward_home), (metal, back_in, back_sum, back_home))
-    ):
+    for path, (src, out, dst) in enumerate(((forward_in, forward_sum, forward_home), (back_in, back_sum, back_home))):
+        routes, name, hit, parts = weighed[path]
         for copy in copies[path]:
             copy.wait_recv()
-        routes, name, hit = combine(path, top, nodes, locals_, meta, src, out)
+        if path == 0:
+            for copy in value_copies:
+                copy.wait_recv()
+        rows_back = src[...].reshape(-1, src.shape[2])
+        total = jnp.dot(parts[0], rows_back, preferred_element_type=F32)
+        total = total + jnp.dot(parts[1], rows_back, preferred_element_type=F32)
+        out[...] = total.astype(BF16).reshape(out.shape)
         me, at, peers, _ = ways[1 - path]
         for step in range(1, len(at)):
             sem = (step, path)
@@ -540,54 +600,160 @@
             gates_home[0] = gates_sum[me]
     for copy in homeward:
         copy.wait()
-    for copy in copies[0] + copies[1] + ring_copies:
+    for copy in copies[0] + copies[1] + value_copies + ring_copies:
         copy.wait_send()
 
 
-def main(chips, nodes, locals_, count, ident, counts, count_sum, toks, cots, metaz, metal, rows, wg, wu, wd, wg2, wu2, wd2):
-    top = metaz.shape[1] // 2
-    _, slots, features = toks.shape
-    wide = 3 * (wg.shape[2] // SUBS)
+def main_shapes(nodes, locals_, rows, features, top):
+    return [((nodes, rows, features), BF16), ((locals_, rows, features), BF16), ((nodes, top, 128), F32)]
+
+
+def main_scratch(chips, nodes, locals_, count, rows, features, hidden, top):
+    wide = 3 * (hidden // SUBS)
     depth = chips // 2
     share = count // chips
     most = max(nodes, locals_)
-    table = (3, chips, 128)
-    forward = (2, locals_, nodes * CAP, features)
-    back = (2, nodes, locals_ * CAP, features)
-    homes = [((nodes, rows, features), BF16), ((locals_, rows, features), BF16), ((nodes, top, 128), F32)]
+    forward, back, _, _, _, _ = (shape for shape, _ in front_shapes(nodes, locals_, features, top))
     dma = pltpu.SemaphoreType.DMA
-    return pl.pallas_call(
-        functools.partial(main_kernel, chips, nodes, locals_),
-        out_shape=[jax.ShapeDtypeStruct(*one) for one in homes],
-        in_specs=[VMEM] * 6 + [ANY] * 3 + [VMEM] * 3,
-        out_specs=[VMEM] * 3,
-        scratch_shapes=[pltpu.VMEM(w.shape, BF16) for w in (wg2, wu2, wd2)]
+    return (
+        [pltpu.VMEM(shape, BF16) for shape in ((features, hidden), (features, hidden), (hidden, features)) * 2]
         + [
+            pltpu.VMEM((2, nodes * locals_ * CAP, count), BF16),
+            pltpu.VMEM((2, 2, count, features), F32),
             pltpu.VMEM((2, 2, count, features), BF16),
             pltpu.VMEM((SUBS, chips, share, wide), F32),
-            pltpu.VMEM(table, F32),
+            pltpu.VMEM((chips, 128), F32),
             pltpu.VMEM((SUBS, chips, share, wide), BF16),
-            pltpu.VMEM((chips, 8, 128), F32),
+            pltpu.VMEM((chips, 1, 128), F32),
             pltpu.VMEM((2, depth, SUBS, share, wide), jnp.int16),
             pltpu.VMEM((2, depth, SUBS, share, wide), jnp.int16),
-            pltpu.VMEM((2, depth) + table, F32),
-            pltpu.VMEM((2, depth) + table, F32),
+            pltpu.VMEM((2, depth, chips, 128), F32),
+            pltpu.VMEM((2, depth, chips, 128), F32),
             pltpu.VMEM(forward, BF16),
             pltpu.VMEM(back, BF16),
-            pltpu.VMEM((locals_, 8, 128), F32),
+            pltpu.VMEM((locals_, 1, 128), F32),
             pltpu.VMEM((2 * locals_,) + forward[2:], BF16),
             pltpu.VMEM((2 * nodes,) + back[2:], BF16),
-            pltpu.VMEM((2 * locals_, 8, 128), F32),
+            pltpu.VMEM((2 * locals_, 1, 128), F32),
         ]
-        + [pltpu.VMEM(*one) for one in homes]
-        + [dma((3,))]
+        + [pltpu.VMEM(*one) for one in main_shapes(nodes, locals_, rows, features, top)]
         + [dma((2, depth, SUBS))] * 4
         + [dma((2, depth))] * 4
         + [dma((2, most, 2))] * 2
         + [dma((locals_, 2))] * 2
-        + [dma((most, 3))] * 2,
-        compiler_params=pltpu.CompilerParams(collective_id=ident, has_side_effects=True, vmem_limit_bytes=LIMIT),
+        + [dma((most, 3))] * 2
+    )
+
+
+def main_kernel(
+    chips, nodes, locals_, counts, count_sum, toks, cots, metaz, metal, wg_own, wu_own, wd_own, wg_twin, wu_twin, wd_twin,
+    forward_home, back_home, gates_home, wsem, wg, wu, wd, wg2, wu2, wd2, *scratch,
+):
+    core, ways, everyone = paths_of(nodes, locals_)
+    _, way = ring_way(chips)
+    hail(everyone + way)
+    sources = (wg_own.at[core], wu_own.at[core], wd_own.at[core], wg_twin, wu_twin, wd_twin)
+    load = []
+    for index, (src, dst) in enumerate(zip(sources, (wg, wu, wd, wg2, wu2, wd2))):
+        load.append(pltpu.make_async_copy(src, dst, wsem.at[index]))
+        load[-1].start()
+
+    def nothing():
+        pass
+
+    def ready_weights():
+        for copy in load:
+            copy.wait()
+
+    main_steps(
+        chips, nodes, locals_, ways, core, nothing, ready_weights, nothing, nothing, lambda: await_all(everyone + way),
+        counts, count_sum, toks, cots, metaz, metal, forward_home, back_home, gates_home,
+        wg, wu, wd, wg2, wu2, wd2, *scratch,
+    )
+
+
+def main(chips, nodes, locals_, count, counts, count_sum, toks, cots, metaz, metal, rows, wg, wu, wd, wg2, wu2, wd2):
+    top = metaz.shape[1]
+    features, hidden = wg2.shape
+    return pl.pallas_call(
+        functools.partial(main_kernel, chips, nodes, locals_),
+        out_shape=[jax.ShapeDtypeStruct(*one) for one in main_shapes(nodes, locals_, rows, features, top)],
+        in_specs=[VMEM] * 6 + [ANY] * 6,
+        out_specs=[VMEM] * 3,
+        scratch_shapes=[pltpu.SemaphoreType.DMA((6,))]
+        + main_scratch(chips, nodes, locals_, count, rows, features, hidden, top),
+        compiler_params=pltpu.CompilerParams(collective_id=2, has_side_effects=True, vmem_limit_bytes=LIMIT),
     )(counts, count_sum, toks, cots, metaz, metal, wg, wu, wd, wg2, wu2, wd2)
+
+
+def whole_kernel(
+    chips, nodes, locals_, tok, cot, gates, routes, wg_own, wu_own, wd_own,
+    forward_home, back_home, gates_home, count_sum,
+    wsem, wsend, wrecv, toks, cots, counts, metaz, metal, meta, tokz, cotl, tok_out, cot_out, count,
+    send, recv, ssend, srecv, csend, crecv, wg, wu, wd, wg2, wu2, wd2, *scratch,
+):
+    core, ways, everyone = paths_of(nodes, locals_)
+    _, twin = other_core()
+    _, way = ring_way(chips)
+    hail(everyone + way)
+    fill_meta(gates, routes, meta)
+    weights = (wg_own, wu_own, wd_own)
+    load, swapped = [], []
+    for index, (src, dst) in enumerate(zip(weights, (wg, wu, wd))):
+        load.append(pltpu.make_async_copy(src.at[core], dst, wsem.at[index]))
+        load[-1].start()
+    await_all(everyone + way)
+
+    def swap():
+        for index, (src, dst) in enumerate(zip(weights, (wg2, wu2, wd2))):
+            swapped.append(push(src.at[1 - core], dst, wsend.at[index], wrecv.at[index], {"dp": twin}))
+
+    numbers, tok_copies, cot_copies, blocks = front_steps(
+        nodes, locals_, ways, core, tok, cot, gates, routes, toks, cots, counts, count_sum, metaz, metal, swap,
+        meta, tokz, cotl, tok_out, cot_out, count, send, recv, ssend, srecv, csend, crecv,
+    )
+
+    def received(copies):
+        for copy in copies:
+            copy.wait_recv()
+
+    def ready_counts():
+        received(numbers)
+        count_sum[...] = jnp.sum(counts[...], axis=0)
+
+    def ready_weights():
+        for copy in load:
+            copy.wait()
+        received(swapped)
+
+    main_steps(
+        chips, nodes, locals_, ways, core, ready_counts, ready_weights, lambda: received(tok_copies),
+        lambda: received(cot_copies), lambda: None,
+        counts, count_sum, toks, cots, metaz, metal, forward_home, back_home, gates_home,
+        wg, wu, wd, wg2, wu2, wd2, *scratch,
+    )
+    for copy in numbers + tok_copies + cot_copies + blocks + swapped:
+        copy.wait_send()
+
+
+def whole(chips, nodes, locals_, count, tok, cot, gates, routes, wg, wu, wd):
+    rows, features = tok.shape
+    top = gates.shape[0]
+    hidden = wg.shape[2]
+    parts = front_shapes(nodes, locals_, features, top)
+    homes = main_shapes(nodes, locals_, rows, features, top)
+    inner = [pltpu.VMEM(*one) for one in parts[:3] + parts[4:]]
+    return pl.pallas_call(
+        functools.partial(whole_kernel, chips, nodes, locals_),
+        out_shape=[jax.ShapeDtypeStruct(*one) for one in homes + [parts[3]]],
+        in_specs=[VMEM] * 4 + [ANY] * 3,
+        out_specs=[VMEM] * 4,
+        scratch_shapes=[pltpu.SemaphoreType.DMA((3,))] * 3
+        + inner
+        + front_scratch(nodes, locals_, rows, features, top)
+        + main_scratch(chips, nodes, locals_, count, rows, features, hidden, top),
+        compiler_params=pltpu.CompilerParams(collective_id=0, has_side_effects=True, vmem_limit_bytes=LIMIT),
+    )(tok, cot, gates, routes, wg, wu, wd)
 
 
 def total_kernel(forward, back, gates, mixed, grads, gates_out):
@@ -609,23 +775,21 @@
 
 
 def body(chips, nodes, locals_, tokens, cotangent, routes, gate_weights, w_gate, w_up, w_down):
-    rows, features = tokens.shape
+    rows = tokens.shape[0]
     slots = nodes * locals_ * CAP
-    toks, cots, counts, count_sum, metaz, metal, *swapped = front(
-        nodes, locals_, tokens, cotangent, gate_weights.T, routes.T, w_gate, w_up, w_down
-    )
-    toks, cots = toks.reshape(2, slots, features), cots.reshape(2, slots, features)
-
-    def sized(count, ident):
-        def call(*operands):
-            return main(chips, nodes, locals_, count, ident, *operands[:6], rows, *operands[6:])
-
-        return call
+    inputs = (tokens, cotangent, gate_weights.T, routes.T, w_gate, w_up, w_down)
+    *sums, count_sum = whole(chips, nodes, locals_, USUAL * chips, *inputs)
+
+    def usual(sums, inputs):
+        return total(*sums)
+
+    def every(sums, inputs):
+        toks, cots, counts, number, metaz, metal, *swapped = front(nodes, locals_, *inputs)
+        weights = (*inputs[4:], *swapped)
+        return total(*main(chips, nodes, locals_, slots, counts, number, toks, cots, metaz, metal, rows, *weights))
 
     crowded = jnp.max(count_sum[2 * locals_ :, :]) > USUAL * chips
-    operands = (counts, count_sum, toks, cots, metaz, metal, w_gate, w_up, w_down, *swapped)
-    sums = lax.cond(crowded, sized(slots, 2), sized(USUAL * chips, 1), *operands)
-    mixed, grads, gates = total(*sums)
+    mixed, grads, gates = lax.cond(crowded, every, usual, tuple(sums), inputs)
     return mixed, grads, gates.T
 
 

time: 120 us -> 110 us (0.917)
  Pallas kernels: 118 us -> 106 us
    pallas_call x2 -> x1, Pallas kernels: 116 us -> 105 us  [whole(): pl.pallas_call(functools.partial(whole_kernel, chips, nodes, locals_), ou...]
where the time goes in v4:
time: 110 us; the launch traced here: 109 us
  Pallas kernels  106 us (96%)
  between operations  1.34 us (1%)
  other arithmetic  1.28 us (1%)
    pallas_call x1, Pallas kernels, whole(): pl.pallas_call(functools.partial(whole_kernel, chips, nodes, locals_), ou...  105 us

profile of v4, /device:TPU:1, one launch (start us, length us, event | category | flops | bytes accessed | tf_op | source)
XLA Modules:
  0.0 109.4 jit_solution(120382057505315024)
XLA Ops:
  0.6 0.0 copy-start.3
  0.6 0.7 copy-done.3
  1.3 0.0 copy-start
  1.3 0.0 copy-start.1
  1.3 0.0 copy-start.2
  1.3 104.6 %shard_map.94 = (bf16[8,48,256]{2,1,0:T(8,128)(2,1)S(1)}, bf16[8,48,256]{2,1,0:T(8,128)(2,1)S(1)}, f32[8,8,128]{2,1,0:T(8,128)}, f32[24,128]{1,0:T(8,128)}) custom-call(bf16[48,256]{1,0:T(8,128)(2,1)} %tok.1, bf16[48,256]{1,0:T(8,128)(2,1)} %cot.1, f32[8,48]{1,0:T(8,128)S(1)} %bitcast.3, s32[8,48]{1,0:T(8,128)} %bitcast.5, bf16[2,256,1024]{2,1,0:T(8,128)(2,1)} %wg_own.1, ...), custom_call_target="tpu_custom_call" | custom-call | tf_op jit(solution)/shard_map/pallas_call | solution.py:746
  106.0 0.0 copy-start.4
  106.0 1.3 %slice_reduce_fusion = f32[]{:T(128)} fusion(f32[24,128]{1,0:T(8,128)} %get-tuple-element.52), kind=kLoop, calls=%fused_computation | loop fusion | flops 1023 | bytes 4100 | tf_op jit(solution)/shard_map/reduce_max | solution.py:791
  107.9 0.0 copy-done
  107.9 0.0 copy-done.1
  107.9 0.0 copy-done.2
  107.9 0.0 copy-done.4
  107.9 1.4 %conditional.1 = ((bf16[48,256]{1,0:T(8,128)(2,1)}, bf16[48,256]{1,0:T(8,128)(2,1)}, f32[8,48]{1,0:T(8,128)})) conditional(s32[]{:T(128)} %convert_element_type.3, (bf16[8,48,256]{2,1,0:T(8,128)(2,1)S(1)}, bf16[8,48,256]{2,1,0:T(8,128)(2,1)S(1)}, f32[8,8,128]{2,1,0:T(8,128)}) %tuple.14, (bf16[48,256]{1,0:T(8,128)(2,1)}, bf16[48,256]{1,0:T(8,128)(2,1)}, ...), branch_computations={%region_1.0_spmd, %region_2.0_spmd} | conditional | bytes 8 | solution.py:792
  108.0 1.4 %branch_0_fun.1 = (bf16[48,256]{1,0:T(8,128)(2,1)}, bf16[48,256]{1,0:T(8,128)(2,1)}, f32[8,48]{1,0:T(8,128)}) custom-call(bf16[8,48,256]{2,1,0:T(8,128)(2,1)S(1)} %get-tuple-element.20.forward, bf16[8,48,256]{2,1,0:T(8,128)(2,1)S(1)} %get-tuple-element.21.back, f32[8,8,128]{2,1,0:T(8,128)} %get-tuple-element.22.gates), custom_call_target="tpu_custom_call" | custom-call | tf_op jit(solution)/shard_map/cond/branch_0_fun/pallas_call | solution.py:768
Async XLA Ops:
  0.6 0.7 copy-start.3
  1.3 106.6 %copy-start = (bf16[2,256,1024]{2,1,0:T(8,128)(2,1)S(1)}, bf16[2,256,1024]{2,1,0:T(8,128)(2,1)}, u32[]{:S(2)}) copy-start(bf16[2,256,1024]{2,1,0:T(8,128)(2,1)} %wg_own.1) | copy-start | bytes 3145732
  1.3 106.6 %copy-start.1 = (bf16[2,256,1024]{2,1,0:T(8,128)(2,1)S(1)}, bf16[2,256,1024]{2,1,0:T(8,128)(2,1)}, u32[]{:S(2)}) copy-start(bf16[2,256,1024]{2,1,0:T(8,128)(2,1)} %wu_own.1) | copy-start | bytes 3145732
  1.3 106.6 %copy-start.2 = (bf16[2,1024,256]{2,1,0:T(8,128)(2,1)S(1)}, bf16[2,1024,256]{2,1,0:T(8,128)(2,1)}, u32[]{:S(2)}) copy-start(bf16[2,1024,256]{2,1,0:T(8,128)(2,1)} %wd_own.1) | copy-start | bytes 3145732
  106.0 2.0 %copy-start.4 = (s32[48,8]{0,1:T(8,128)S(1)}, s32[48,8]{0,1:T(8,128)}, u32[]{:S(2)}) copy-start(s32[48,8]{0,1:T(8,128)} %param.11) | copy-start | bytes 4612
